TPU v7x, 256 devices: a whole 4x4x8 slice. The times are simulated.
256 devices in a mesh: exp: 2 (over z_lo), tile: 8 (over x, core), depth: 16 (over y, z_hi).
Axes of the slice: x: 4, y: 4, z: 8 (z_hi: 4, z_lo: 2; z = z_hi * 2 + z_lo), core: 2. Of those that a mesh axis runs over, the one named last changes fastest.
Arguments:
- images: float32 [2, 4, 1024, 512], P('exp', None, 'tile'), may hold values from 0.25 to 4
- offsets: int32 [4, 64], P(None, 'depth'), may hold values from -6 to 6
- fractions: float32 [4, 64], P(None, 'depth'), may hold values from 0 to 1
- shifts: int32 [128, 3], P(('tile', 'depth')), may hold values from -8 to 7
Outputs:
- correlation: float32 [128, 64, 4096], P(('tile', 'depth'), 'exp')
All inputs are finite; a program needn't handle non-finite values.
Results may differ from a plain program's by a relative error of at most 0.0003.
Values sent between devices are 32-bit elements; how exact they have to be, the bound alone decides.
A program may use at most 64 MiB of HBM per device.

v0:
```python
import math

import jax
import jax.numpy as jnp
from jax import lax
from jax.sharding import PartitionSpec as P

BRICK = 64
HALO = 8
ITERS = 2


highest = lax.Precision.HIGHEST
spectral_floor = 0.01


def with_halo(cells, sides, width):
    for axis, dim in sides:
        count = lax.axis_size(axis)
        head = lax.slice_in_dim(cells, 0, width, axis=dim)
        tail = lax.slice_in_dim(cells, cells.shape[dim] - width, cells.shape[dim], axis=dim)
        cells = jnp.concatenate(
            [
                lax.ppermute(tail, axis, [(i, (i + 1) % count) for i in range(count)]),
                cells,
                lax.ppermute(head, axis, [((i + 1) % count, i) for i in range(count)]),
            ],
            axis=dim,
        )
    return cells


def partner_2(value, axis, apart):
    mask = 2**apart
    pairs = [(source, source ^ mask) for source in range(lax.axis_size(axis))]
    return lax.ppermute(value, axis, pairs)


def tent_value(distance, fraction):
    return jnp.maximum(0.0, 1.0 - jnp.abs(distance - fraction) / 1.5)


def dft_tables(length):
    wave = jnp.arange(length, dtype=jnp.int32)
    turns = wave[:, None] * wave[None, :] % length
    angle = turns.astype(jnp.float32) * (2.0 * math.pi / length)
    factor = 1.0 / math.sqrt(length)
    return (jnp.cos(angle) * factor, jnp.sin(angle) * factor)


def along_x(table_cos, table_sin, stacked, brick, sign):
    cos_part = jnp.einsum(
        "kx,zxm->zkm", table_cos, stacked, precision=highest, preferred_element_type=jnp.float32
    )
    sin_part = jnp.einsum(
        "kx,zxm->zkm", table_sin, stacked, precision=highest, preferred_element_type=jnp.float32
    )
    re_part = cos_part[..., :brick] + sign * sin_part[..., brick:]
    im_part = cos_part[..., brick:] - sign * sin_part[..., :brick]
    return jnp.concatenate([re_part, im_part], axis=-1)


def cross_power(first, second, kz_index, shift_row, brick):
    re_one = first[..., :brick]
    im_one = first[..., brick:]
    re_two = second[..., :brick]
    im_two = second[..., brick:]
    prod_re = re_one * re_two + im_one * im_two
    prod_im = re_one * im_two - im_one * re_two
    scale = jnp.maximum(
        jnp.sqrt((re_one * re_one + im_one * im_one) * (re_two * re_two + im_two * im_two)),
        spectral_floor,
    )
    wave = jnp.arange(brick, dtype=jnp.int32)
    turns = (
        kz_index[:, None, None] * shift_row[0]
        + wave[None, :, None] * shift_row[1]
        + wave[None, None, :] * shift_row[2]
    ) % brick
    angle = turns.astype(jnp.float32) * (2.0 * math.pi / brick)
    cos_t = jnp.cos(angle)
    sin_t = jnp.sin(angle)
    out_re = (prod_re * cos_t - prod_im * sin_t) / scale
    out_im = (prod_re * sin_t + prod_im * cos_t) / scale
    anchor = (
        (kz_index[:, None, None] == 0) & (wave[None, :, None] == 0) & (wave[None, None, :] == 0)
    )
    out_re = jnp.where(anchor, 0.0, out_re)
    out_im = jnp.where(anchor, 0.0, out_im)
    return jnp.concatenate([out_re, out_im], axis=-1)


def per_device(images, offsets, fractions, shifts):
    cameras, width, rows_y = (images.shape[1], images.shape[2], images.shape[3])
    slab = offsets.shape[1]
    brick = BRICK
    padded_width = width + 2 * HALO
    log_images = jnp.log(images[0])
    tap_list = jnp.arange(-2, 4).astype(jnp.float32)
    tent_sum = jnp.sum(tent_value(tap_list[None, None, :], fractions[..., None]), axis=-1)
    local_pos = jnp.arange(width, dtype=jnp.int32)
    padded_pos = jnp.arange(padded_width, dtype=jnp.int32)
    fwd_dist = (
        local_pos[None, :, None, None]
        - padded_pos[None, None, None, :]
        + HALO
        - offsets[:, None, :, None]
    )
    fwd_table = (
        tent_value(fwd_dist.astype(jnp.float32), fractions[:, None, :, None])
        / tent_sum[:, None, :, None]
        / brick
    )
    fwd_table = fwd_table.reshape(cameras * width, slab * padded_width)
    back_dist = (
        padded_pos[None, None, None, :]
        - HALO
        - local_pos[None, :, None, None]
        - offsets.T[:, None, :, None]
    )
    back_table = (
        tent_value(back_dist.astype(jnp.float32), fractions.T[:, None, :, None])
        / tent_sum.T[:, None, :, None]
        / cameras
    )
    back_table = back_table.reshape(slab * width, cameras * padded_width)
    log_volume = jnp.zeros((slab, width, rows_y), jnp.float32)
    for iteration in range(ITERS):
        volume = jnp.exp(log_volume)
        padded = with_halo(volume, (("tile", 1),), HALO)
        partial_value = jnp.dot(
            fwd_table,
            padded.reshape(slab * padded_width, rows_y),
            precision=highest,
            preferred_element_type=jnp.float32,
        )
        partial_value = partial_value.reshape(cameras, width, rows_y)
        totals = lax.psum(partial_value, "depth")
        ratio = log_images - jnp.log(totals)
        ratio_ext = with_halo(ratio, (("tile", 1),), HALO)
        update = jnp.dot(
            back_table,
            ratio_ext.reshape(cameras * padded_width, rows_y),
            precision=highest,
            preferred_element_type=jnp.float32,
        )
        log_volume = log_volume + update.reshape(slab, width, rows_y)
    volume = jnp.exp(log_volume)
    bricks_x = width // brick
    bricks_y = rows_y // brick
    blocks = volume.reshape(slab, bricks_x, brick, bricks_y, brick).transpose(1, 3, 0, 2, 4)
    blocks = blocks.reshape(bricks_x * bricks_y, slab, brick * brick)
    table_cos, table_sin = dft_tables(brick)
    depth_table = jnp.concatenate([table_cos, -table_sin], axis=0)
    z_spec = jnp.einsum(
        "kz,bzm->bkm",
        depth_table,
        lax.all_to_all(blocks, "depth", split_axis=0, concat_axis=1, tiled=True),
        precision=highest,
        preferred_element_type=jnp.float32,
    )
    z_spec = z_spec.reshape(2, brick, brick, brick)
    y_input = jnp.concatenate([z_spec[0], z_spec[1]], axis=-1)
    fwd_y = jnp.concatenate(
        [
            jnp.concatenate([table_cos, -table_sin], axis=1),
            jnp.concatenate([table_sin, table_cos], axis=1),
        ],
        axis=0,
    )
    inv_y = jnp.concatenate(
        [
            jnp.concatenate([table_cos, table_sin], axis=1),
            jnp.concatenate([-table_sin, table_cos], axis=1),
        ],
        axis=0,
    )
    y_spec = jnp.dot(
        y_input.reshape(-1, 2 * brick), fwd_y, precision=highest, preferred_element_type=jnp.float32
    )
    spectrum = along_x(table_cos, table_sin, y_spec.reshape(brick, brick, 2 * brick), brick, 1.0)
    exp_side = lax.axis_index("exp")
    plane_rows = brick // lax.axis_size("exp")
    shift_row = shifts[0]
    partner = partner_2(spectrum, "exp", 0)
    first = jnp.where(exp_side == 0, spectrum, partner)
    second = jnp.where(exp_side == 0, partner, spectrum)
    kz_index = jnp.arange(brick, dtype=jnp.int32)
    cross = cross_power(first, second, kz_index, shift_row, brick)
    count = cross.shape[0]
    y_back = jnp.dot(
        cross.reshape(-1, 2 * brick), inv_y, precision=highest, preferred_element_type=jnp.float32
    )
    inverted = along_x(table_cos, table_sin, y_back.reshape(count, brick, 2 * brick), brick, -1.0)
    stacked = jnp.concatenate([inverted[..., :brick], inverted[..., brick:]], axis=0)
    cos_rows = lax.dynamic_slice_in_dim(table_cos, exp_side * plane_rows, plane_rows, 0)
    sin_rows = lax.dynamic_slice_in_dim(table_sin, exp_side * plane_rows, plane_rows, 0)
    z_table = jnp.concatenate([cos_rows, -sin_rows], axis=1)
    result = jnp.einsum(
        "zk,kxy->zxy", z_table, stacked, precision=highest, preferred_element_type=jnp.float32
    )
    return result.reshape(1, plane_rows, brick * brick)


def solution(mesh):
    placed = (
        P("exp", None, "tile", None),
        P(None, "depth"),
        P(None, "depth"),
        P(("tile", "depth"), None),
    )
    return jax.shard_map(
        per_device,
        mesh=mesh,
        in_specs=placed,
        out_specs=P(("tile", "depth"), "exp", None),
        check_vma=False,
    )
```

profile of v0, /device:TPU:2, one launch (start us, length us, event | category | flops | bytes accessed | tf_op | source)
XLA Modules:
  0.0 553.5 jit_solution(8956696591463915781)
XLA Ops:
  10.2 4.6 convolution_bitcast_fusion.8
  15.4 174.6 %all-reduce.3.cloned.1.call-done = f32[4,128,512]{2,1,0:T(8,128)} async-done(((f32[4,128,512]{2,1,0:T(8,128)}), f32[4,128,512]{2,1,0:T(8,128)}) %all-reduce.3.cloned.1.call-update) | async-done | bytes 1048592 | tf_op jit(solution)/shard_map/psum | solution.py:138
  195.2 4.0 fusion.110
  202.9 4.0 convolution_bitcast_fusion.6
  206.9 170.5 %all-reduce.5.cloned.1.call-done = f32[4,128,512]{2,1,0:T(8,128)} async-done(((f32[4,128,512]{2,1,0:T(8,128)}), f32[4,128,512]{2,1,0:T(8,128)}) %all-reduce.5.cloned.1.call-update) | async-done | bytes 1048592 | tf_op jit(solution)/shard_map/psum | solution.py:138
  380.6 1.9 collective-permute-done.6
  382.6 3.0 fusion.16
  387.7 14.5 %reshape.256 = f32[16,4,4096]{2,0,1:T(8,128)S(1)} reshape(f32[2,8,4,64,64]{4,3,1,0,2:T(8,128)} %bitcast.82) | data formatting | bytes 2097152 | tf_op jit(solution)/shard_map/reshape | solution.py:152
  403.9 5.3 all-to-all-start
  409.5 30.7 %all-to-all-done = f32[16,4,4096]{2,1,0:T(4,128)S(1)} async-done(((f32[16,4,4096]{2,1,0:T(4,128)}), f32[16,4,4096]{2,1,0:T(4,128)S(1)}, u32[]{:S(2)}, u32[]{:S(2)}) %all-to-all-start) | async-done | bytes 1048608 | tf_op jit(solution)/shard_map/all_to_all | solution.py:158
  443.5 2.0 concatenate.60
  445.6 2.2 concatenate.61
  447.7 3.6 fusion.7
  451.3 2.2 convolution_bitcast_fusion.3
  453.5 2.2 convolution_bitcast_fusion.4
  456.8 2.0 pad_maximum_fusion.1
  461.6 45.6 %collective-permute-done.8 = f32[64,64,128]{2,1,0:T(8,128)} collective-permute-done((f32[64,64,128]{2,1,0:T(8,128)}, f32[64,64,128]{2,1,0:T(8,128)}, u32[]{:S(2)}, u32[]{:S(2)}) %collective-permute-start.8) | collective-permute-done | bytes 2097184 | tf_op jit(solution)/shard_map/ppermute | solution.py:36
  507.2 2.9 broadcast_select_fusion.1
  510.1 11.9 %and_select_fusion.1 = (f32[64,64,64]{2,1,0:T(8,128)S(1)}, f32[64,64,64]{2,1,0:T(8,128)S(1)}, f32[64,64,64]{2,1,0:T(8,128)S(1)}, f32[64,64,64]{2,1,0:T(8,128)S(1)}) fusion(s32[64]{0:T(128)S(1)} %iota_multiply_fusion, s32[64,64]{1,0:T(8,128)S(1)} %broadcast_add_fusion, pred[64]{0:T(512)(128)(4,1)S(1)} %iota_compare_fusion, ...), kind=kLoop, calls=%fused_computation.10 | loop fusion | flops 8912896 | bytes 8409408 | tf_op jit(solution)/shard_map/jit(_where)/select_n | solution.py:88
  522.0 9.7 %and_select_fusion = f32[64,64,64]{2,1,0:T(8,128)S(1)} fusion(f32[64,64,64]{2,1,0:T(8,128)S(1)} %get-tuple-element.8, f32[64,64,64]{2,1,0:T(8,128)S(1)} %get-tuple-element.7, f32[64,64,64]{2,1,0:T(8,128)S(1)} %get-tuple-element.6, s32[64]{0:T(128)S(1)} %iota_multiply_fusion, s32[64,64]{1,0:T(8,128)S(1)} %broadcast_add_fusion, ...), kind=kLoop, calls=%fused_computation.9 | loop fusion | flops 5242880 | bytes 4215104 | tf_op jit(solution)/shard_map/jit(_where)/select_n | solution.py:89
  531.7 2.0 fusion.11
  533.7 2.2 convolution_bitcast_fusion.1
  535.9 2.2 convolution_bitcast_fusion.2
  540.1 4.6 fusion
  (69 shorter events, 31.4 us)
Async XLA Ops:
  6.5 183.4 %all-reduce.3.cloned.1.call-start = ((), (), s32[]{:S(2)}) async-start(), calls=%async_computation.1 | async-start | bytes 2097152 | tf_op jit(solution)/shard_map/psum | solution.py:138
  6.5 3.7 collective-permute-start
  6.6 3.7 collective-permute-start.1
  9.2 180.7 %copy-start.1 = (f32[1,4,128,512]{3,2,1,0:T(8,128)S(1)}, f32[1,4,128,512]{3,2,1,0:T(8,128)}, u32[]{:S(2)}) copy-start(f32[1,4,128,512]{3,2,1,0:T(8,128)} %param.4) | copy-start | bytes 3145732
  14.9 178.5 %copy-start.4 = (s32[4,4]{1,0:T(4,128)S(1)}, s32[4,4]{1,0:T(4,128)}, u32[]{:S(2)}) copy-start(s32[4,4]{1,0:T(4,128)} %param.5) | copy-start | bytes 196
  14.9 178.6 %copy-start.2 = (f32[4,4]{1,0:T(4,128)S(1)}, f32[4,4]{1,0:T(4,128)}, u32[]{:S(2)}) copy-start(f32[4,4]{1,0:T(4,128)} %param.6) | copy-start | bytes 196
  14.9 362.4 %all-reduce.5.cloned.1.call-start = ((), (), s32[]{:S(2)}) async-start(), calls=%async_computation.2 | async-start | bytes 2097152 | tf_op jit(solution)/shard_map/psum | solution.py:138
  191.4 3.7 collective-permute-start.2
  191.5 3.7 collective-permute-start.3
  199.2 3.7 collective-permute-start.4
  200.8 2.1 collective-permute-start.5
  206.8 175.8 %copy-start.5 = (f32[4,128,512]{2,1,0:T(8,128)S(1)}, f32[4,128,512]{2,1,0:T(8,128)}, u32[]{:S(2)}) copy-start(f32[4,128,512]{2,1,0:T(8,128)} %get-tuple-element.27) | copy-start | bytes 3145732
  378.9 3.7 collective-permute-start.6
  378.9 3.7 collective-permute-start.7
  403.9 36.3 %all-to-all-start = ((f32[16,4,4096]{2,1,0:T(4,128)}), f32[16,4,4096]{2,1,0:T(4,128)S(1)}, u32[]{:S(2)}, u32[]{:S(2)}) async-start(f32[16,4,4096]{2,1,0:T(4,128)} %copy.33), calls=%async_computation | async-start | bytes 2097152 | tf_op jit(solution)/shard_map/all_to_all | solution.py:158
  456.8 2.0 copy-start
  456.8 2.0 copy-start.3
  458.8 48.4 %collective-permute-start.8 = (f32[64,64,128]{2,1,0:T(8,128)}, f32[64,64,128]{2,1,0:T(8,128)}, u32[]{:S(2)}, u32[]{:S(2)}) collective-permute-start(f32[64,64,128]{2,1,0:T(8,128)} %pad_maximum_fusion.1), channel_id=1, source_target_pairs={{0,128},{128,0},{1,129},{129,1},{2,130},{130,2},{3,131},{131,3},{4... | collective-permute-start | bytes 6291464 | tf_op jit(solution)/shard_map/ppermute | solution.py:36
Sparse Core Ops, SparseCore 0:
  15.0 174.8 all-reduce.2
  207.0 170.3 all-reduce.4
where the time goes:
time: 557 us; the launch traced here: 553 us
  waiting for transfers between devices  428 us (77%)
  matrix products  36.3 us (7%)
  other arithmetic  35.9 us (6%)
  local copies, waits for them, and re-layouts  26.8 us (5%)
  between operations  13.9 us (2%)
  starting transfers between devices  12.8 us (2%)
    psum x2, waiting for transfers between devices, per_device(): totals = lax.psum(partial_value, 'depth')  345 us
    ppermute x1, waiting for transfers between devices, partner_2(): return lax.ppermute(value, axis, pairs)  45.6 us
    all_to_all x1, waiting for transfers between devices, per_device(): lax.all_to_all(blocks, 'depth', split_axis=0, concat_axis=1, tiled=True)  30.7 us
    reshape x2, local copies, waits for them, and re-layouts, per_device(): blocks = blocks.reshape(bricks_x * bricks_y, slab, brick * brick)  16.2 us
    select_n x1, other arithmetic, cross_power(): out_re = jnp.where(anchor, 0.0, out_re)  11.9 us
  transfers between devices with their start and end apart: 12, of which 8 were waited for; matrix products, arithmetic and copies ran while one was open for 1% of the time, Pallas kernels for 0%

commit v1 on v0

v1 whole, which is shorter than its diff:
```python
import functools
import math

import jax
import jax.numpy as jnp
import ml_dtypes
import numpy as np
from jax import lax
from jax.experimental import pallas as pl
from jax.experimental.pallas import tpu as pltpu
from jax.sharding import PartitionSpec as P

MESH = pl.DeviceIdType.MESH
BRICK = 64
LANES = 128
EDGE = 24
COLS_R = BRICK + 2 * EDGE
COLS_V = BRICK + 32
COLS_U = BRICK + 16
MAIN = BRICK + EDGE
PEERS = 16
FLOOR = 0.01
F32 = jnp.float32
BF16 = jnp.bfloat16


def exchange_kernel(off_ref, frac_ref, img_ref, raw_ref, par_ref, tile_ref, par_send, par_recv, send, recv, local):
    e = lax.axis_index("exp")
    t = lax.axis_index("tile")
    d = lax.axis_index("depth")
    tiles = lax.axis_size("tile")
    other = 1 - e
    half = d // 8
    d_far = (d // 4) * 4 + lax.rem(lax.rem(d, 4) + 3 - 2 * e, 4)
    t_to = lax.rem(t + 1 - 2 * half + tiles, tiles)
    t_from = lax.rem(t - 1 + 2 * half + tiles, tiles)

    def lanes_of(depth):
        return pl.ds(pl.multiple_of(lax.rem(depth, 8) // 2 * LANES, LANES), LANES)

    barrier = pltpu.get_barrier_semaphore()
    partners = [(e, t, lax.rem(d + k, PEERS)) for k in range(1, PEERS)]
    partners += [(other, t, d), (other, t, d_far)]
    partners += [(e, t_to, d), (other, t_to, d), (e, t_from, d), (other, t_from, d)]
    for partner in partners:
        pl.semaphore_signal(barrier, inc=1, device_id=partner, device_id_type=MESH)

    main_src = pl.ds(pl.multiple_of((BRICK - EDGE) * half, 8), MAIN)
    main_dst = pl.ds(pl.multiple_of(EDGE * (1 - half), 8), MAIN)
    strip_src = pl.ds(pl.multiple_of((2 * BRICK - EDGE) * (1 - half), 8), EDGE)
    strip_dst = pl.ds(pl.multiple_of(MAIN * half, 8), EDGE)

    own = pltpu.make_async_copy(
        img_ref.at[0, :, main_src, lanes_of(d)], raw_ref.at[e, :, main_dst, :], local.at[0]
    )
    own.start()

    row = lax.broadcasted_iota(jnp.int32, (8, LANES), 0)
    cam = lax.broadcasted_iota(jnp.int32, (8, LANES), 1) % 4
    tile = jnp.zeros((8, LANES), F32)
    for c in range(4):
        for z in range(4):
            tile = jnp.where((row == z) & (cam == c), off_ref[c, z].astype(F32), tile)
            tile = jnp.where((row == z + 4) & (cam == c), frac_ref[c, z], tile)
    tile_ref[...] = tile

    own_par = pltpu.make_async_copy(tile_ref, par_ref.at[d], local.at[1])
    own_par.start()

    pl.semaphore_wait(barrier, len(partners))

    copies = []
    for index, (target_e, target_d) in enumerate([(e, d), (other, d)]):
        copies.append(
            pltpu.make_async_remote_copy(
                src_ref=img_ref.at[0, :, strip_src, lanes_of(target_d)],
                dst_ref=raw_ref.at[e, :, strip_dst, :],
                send_sem=send.at[2 + index],
                recv_sem=recv.at[2 + index],
                device_id=(target_e, t_to, target_d),
                device_id_type=MESH,
            )
        )
    for index, target_d in enumerate([d, d_far]):
        cams = pl.ds(2 * index, 2)
        copies.append(
            pltpu.make_async_remote_copy(
                src_ref=img_ref.at[0, cams, main_src, lanes_of(target_d)],
                dst_ref=raw_ref.at[e, cams, main_dst, :],
                send_sem=send.at[index],
                recv_sem=recv.at[index],
                device_id=(other, t, target_d),
                device_id_type=MESH,
            )
        )
    for k in range(1, PEERS):
        copies.append(
            pltpu.make_async_remote_copy(
                src_ref=tile_ref,
                dst_ref=par_ref.at[d],
                send_sem=par_send.at[k],
                recv_sem=par_recv.at[k],
                device_id=(e, t, lax.rem(d + k, PEERS)),
                device_id_type=MESH,
            )
        )
    for copy in copies:
        copy.start()
    own.wait()
    own_par.wait()
    for copy in copies:
        copy.wait()


def exchange(images, offsets, fractions):
    smem = pl.BlockSpec(memory_space=pltpu.SMEM)
    anywhere = pl.BlockSpec(memory_space=pl.ANY)
    return pl.pallas_call(
        exchange_kernel,
        out_shape=[
            jax.ShapeDtypeStruct((2, 4, COLS_R, LANES), F32),
            jax.ShapeDtypeStruct((PEERS, 8, LANES), F32),
        ],
        in_specs=[smem, smem, anywhere],
        out_specs=[anywhere, anywhere],
        scratch_shapes=[
            pltpu.VMEM((8, LANES), F32),
            pltpu.SemaphoreType.DMA((PEERS,)),
            pltpu.SemaphoreType.DMA((PEERS,)),
            pltpu.SemaphoreType.DMA((4,)),
            pltpu.SemaphoreType.DMA((4,)),
            pltpu.SemaphoreType.DMA((2,)),
        ],
        compiler_params=pltpu.CompilerParams(collective_id=0, has_side_effects=True),
    )(offsets, fractions, images)


def split(value):
    high = value.astype(BF16)
    low = (value - high.astype(F32)).astype(BF16)
    return high, low


def stack_rows(value):
    high, low = split(value)
    return jnp.concatenate([high, low, high], axis=0)


def stack_lanes(value):
    high, low = split(value)
    return jnp.concatenate([high, low, high], axis=1)


def twice(value):
    high, low = split(value)
    return jnp.concatenate([high, low[:, :BRICK]], axis=1)


def dot(left, right):
    return jnp.dot(left, right, preferred_element_type=F32)


def turn_cos(turns):
    return jnp.cos((turns & (BRICK - 1)).astype(F32) * (2.0 * math.pi / BRICK)) * 0.125


def iota(shape, axis):
    return lax.broadcasted_iota(jnp.int32, shape, axis)


def compute_kernel(
    shift_ref, raw_ref, par_ref, fz_ref, ty_ref, cs_ref, out_ref, r8, rh, rl, g, a8, uh, ul, zs, qs
):
    e = lax.axis_index("exp")
    odd = lax.rem(lax.axis_index("depth"), 2)
    sz, sx, sy = shift_ref[0, 0], shift_ref[0, 1], shift_ref[0, 2]

    r = iota((2 * BRICK, LANES), 0)
    c = iota((2 * BRICK, LANES), 1)
    inv_y = turn_cos((r % BRICK) * (c % BRICK + sy) + 16 * (r // BRICK - c // BRICK))
    y_high, y_low = split(inv_y)
    tiy = jnp.concatenate([y_high, y_high, y_low], axis=0)
    x_of = 2 * (r % (BRICK // 2)) + (r % BRICK) // (BRICK // 2)
    tix = twice(turn_cos((c % BRICK) * (x_of + sx) - 16 * (r // BRICK)))
    r = iota((BRICK // 2, LANES), 0)
    c = iota((BRICK // 2, LANES), 1) % BRICK
    kz = jnp.where(c > 32, c - 32, c)
    weight = jnp.where((kz == 0) | (kz == 32), 1.0, 2.0)
    tiz = twice(weight * turn_cos(kz * (r + 32 * e + sz) + jnp.where(c > 32, 16, 0)))

    sub = iota((8, LANES), 0)
    offs, fracs = [], []
    for i in range(PEERS // 2):
        a, b = par_ref[2 * i], par_ref[2 * i + 1]
        offs.append(jnp.where(sub < 4, a, pltpu.roll(b, 4, 0)))
        fracs.append(jnp.where(sub < 4, pltpu.roll(a, 4, 0), b))
    off = jnp.concatenate(offs, axis=0)
    frac = jnp.concatenate(fracs, axis=0)
    s_of = iota((BRICK, LANES), 1) % BRICK // 4 - 7

    def tent(distance):
        return jnp.maximum(0.0, 1.0 - jnp.abs(distance - frac) / 1.5)

    total = tent(-2.0)
    for tap in range(-1, 4):
        total = total + tent(float(tap))
    weights = tent(s_of.astype(F32) - off) / total * 0.25
    back = twice(weights)
    turned = jnp.concatenate([weights, weights], axis=0).T[:BRICK] * 0.0625
    forward = twice(turned)
    ones = jnp.sum(turned[:, :BRICK], axis=1, keepdims=True)
    first = ones[0:8]
    for i in range(1, 8):
        first = first + ones[8 * i : 8 * i + 8]
    first = first + pltpu.roll(jnp.broadcast_to(first, (8, LANES)), 4, 0)
    log_first = jnp.log(first)

    low_lane = iota((COLS_R, LANES), 1) < BRICK
    pick = low_lane != (odd == 1)
    is_odd = odd == 1
    for cam in range(4):
        one, two = raw_ref[0, cam], raw_ref[1, cam]
        kept = jnp.where(is_odd, two, one)
        moved = jnp.where(is_odd, one, two)
        both = jnp.where(pick, kept, pltpu.roll(moved, BRICK, 1))
        ratio = jnp.log(both) - log_first[cam : cam + 1, :]
        r8[cam * COLS_R : (cam + 1) * COLS_R, :] = ratio
        r8[(cam + 4) * COLS_R : (cam + 5) * COLS_R, :] = pltpu.roll(ratio, COLS_R - 1, 0)

    for x in range(COLS_R - 2):
        col = jnp.concatenate(
            [r8[pl.ds(x, 8, stride=COLS_R), :], r8[pl.ds(x + 2, 8, stride=COLS_R), :]], axis=0
        )
        high, low = split(col)
        rh[:, x * LANES : (x + 1) * LANES] = high
        rl[:, x * LANES : (x + 1) * LANES] = low

    def windows(high_ref, low_ref, x):
        def of(ref):
            return [ref[:, pl.ds(pl.multiple_of((x + 1 + 4 * q) * LANES, LANES), 2 * LANES)] for q in range(4)]

        high = of(high_ref)
        return jnp.concatenate(high + of(low_ref) + high, axis=0)

    def second(i, carry):
        x = 2 * i
        volume = jnp.exp(dot(back, windows(rh, rl, x)))
        g[:, pl.ds(pl.multiple_of(x * LANES, LANES), 2 * LANES)] = dot(forward, stack_rows(volume))
        return carry

    lax.fori_loop(0, COLS_V // 2, second, 0)

    chunk = 8
    for u in range(0, COLS_U, chunk):
        n = (chunk + 1) * LANES

        def group(row, shift):
            total = None
            for q in range(4):
                start = (u + shift + 12 - 4 * q) * LANES
                part = g[16 * q + row : 16 * q + row + 8, start : start + n]
                total = part if total is None else total + part
            return total

        pairs = group(0, 2) + group(8, 0)
        proj = pairs[:, LANES:] + pltpu.roll(pairs[:, : chunk * LANES], 4, 0)
        log_proj = jnp.log(proj)
        for i in range(chunk):
            ratio = r8[pl.ds(u + i + 16, 8, stride=COLS_R), :]
            a8[:, (u + i) * LANES : (u + i + 1) * LANES] = (
                2.0 * ratio + log_first - log_proj[:, i * LANES : (i + 1) * LANES]
            )

    def column(u):
        return a8[:, u * LANES : (u + 1) * LANES]

    def pair(u):
        return jnp.where(sub < 4, column(u), pltpu.roll(column(u + 1), 4, 0))

    for u in range(COLS_U - 3):
        high, low = split(jnp.concatenate([pair(u), pair(u + 2)], axis=0))
        uh[:, u * LANES : (u + 1) * LANES] = high
        ul[:, u * LANES : (u + 1) * LANES] = low

    fz = fz_ref[...]

    def third(i, carry):
        x = 2 * i
        volume = jnp.exp(dot(back, windows(uh, ul, x)))
        spec = dot(fz, stack_rows(volume))
        start = pl.multiple_of(x * BRICK, BRICK)
        zs[pl.ds(start, BRICK), :] = spec[:, :LANES]
        zs[pl.ds(start + BRICK, BRICK), :] = spec[:, LANES:]
        return carry

    lax.fori_loop(0, BRICK // 2, third, 0)

    ty = ty_ref[...]
    cs = cs_ref[...]
    low_half = iota((BRICK, LANES), 1) < BRICK
    low_quarter = iota((BRICK // 2, LANES), 1) < BRICK
    sign = jnp.where(low_half, -1.0, 1.0)
    row_zero = (iota((BRICK, LANES), 0) == 0) & (iota((BRICK, LANES), 1) % BRICK == 0)

    def plane(kz):
        inner = (kz > 0) & (kz < 32)
        im_row = jnp.where(inner, 32 + kz, kz)
        re = zs[pl.ds(kz, BRICK, stride=BRICK), :]
        im = zs[pl.ds(im_row, BRICK, stride=BRICK), :]
        im = jnp.where(inner, im, 0.0)
        spec = dot(stack_lanes(jnp.concatenate([re, im], axis=1)), ty)
        spec = dot(cs, stack_rows(spec))
        s_re = spec[:BRICK, :LANES] + spec[BRICK:, LANES:]
        s_im = spec[:BRICK, LANES:] - spec[BRICK:, :LANES]
        m_re = pltpu.roll(s_re, BRICK, 1)
        m_im = pltpu.roll(s_im, BRICK, 1)
        inv = jnp.minimum(
            lax.rsqrt((s_re * s_re + s_im * s_im) * (m_re * m_re + m_im * m_im)), 1.0 / FLOOR
        )
        prod = jnp.where(low_half, s_re * m_re + s_im * m_im, s_im * m_re - s_re * m_im)
        cross = jnp.where(row_zero & (kz == 0), 0.0, prod * inv)
        back_y = dot(stack_lanes(cross), tiy)
        back_x = dot(tix, stack_rows(back_y))
        corr = back_x[:BRICK] + sign * pltpu.roll(back_x[BRICK:], BRICK, 1)
        even, odd_x = corr[: BRICK // 2], corr[BRICK // 2 :]
        qs[pl.ds(kz, BRICK // 2, stride=BRICK), :] = jnp.where(
            low_quarter, even, pltpu.roll(odd_x, BRICK, 1)
        )

        @pl.when(inner)
        def _():
            qs[pl.ds(im_row, BRICK // 2, stride=BRICK), :] = jnp.where(
                low_quarter, pltpu.roll(even, BRICK, 1), odd_x
            )

    def planes(i, carry):
        for k in range(3):
            plane(3 * i + k)
        return carry

    lax.fori_loop(0, 11, planes, 0)

    def last(i, carry):
        start = pl.multiple_of(2 * i * BRICK, BRICK)
        data = jnp.concatenate([qs[pl.ds(start, BRICK), :], qs[pl.ds(start + BRICK, BRICK), :]], axis=1)
        out_ref[:, pl.ds(pl.multiple_of(2 * i * LANES, LANES), 2 * LANES)] = dot(tiz, stack_rows(data))
        return carry

    lax.fori_loop(0, BRICK // 4, last, 0)


def halves(table):
    high = table.astype(ml_dtypes.bfloat16)
    low = (table - high.astype(np.float64)).astype(ml_dtypes.bfloat16)
    return high, low


@functools.cache
def tables():
    wave = np.arange(BRICK)
    angle = 2.0 * np.pi / BRICK * (wave[:, None] * wave[None, :] % BRICK)
    cos, sin = np.cos(angle) / 8.0, np.sin(angle) / 8.0
    high, low = halves(np.concatenate([cos[:33], -sin[1:32]], axis=0))
    fz = np.concatenate([high, high, low], axis=1)
    eye = np.eye(2)
    cos2, sin2 = np.kron(eye, cos), np.kron(eye, sin)
    high, low = halves(np.block([[cos2, -sin2], [sin2, cos2]]))
    ty = np.concatenate([high, high, low], axis=0)
    high, low = halves(np.concatenate([cos, sin], axis=0))
    cs = np.concatenate([high, high, low], axis=1)
    return fz, ty, cs


def compute(shifts, raw, par):
    vmem = pl.BlockSpec(memory_space=pltpu.VMEM)
    return pl.pallas_call(
        compute_kernel,
        out_shape=jax.ShapeDtypeStruct((BRICK // 2, BRICK * BRICK), F32),
        in_specs=[pl.BlockSpec(memory_space=pltpu.SMEM)] + [vmem] * 5,
        out_specs=vmem,
        scratch_shapes=[
            pltpu.VMEM((8 * COLS_R, LANES), F32),
            pltpu.VMEM((16, COLS_R * LANES), BF16),
            pltpu.VMEM((16, COLS_R * LANES), BF16),
            pltpu.VMEM((BRICK, COLS_V * LANES), F32),
            pltpu.VMEM((8, COLS_U * LANES), F32),
            pltpu.VMEM((16, COLS_U * LANES), BF16),
            pltpu.VMEM((16, COLS_U * LANES), BF16),
            pltpu.VMEM((BRICK * BRICK, LANES), F32),
            pltpu.VMEM((BRICK * BRICK // 2, LANES), F32),
        ],
        compiler_params=pltpu.CompilerParams(vmem_limit_bytes=40 * 1024 * 1024),
    )(shifts, raw, par, *[jnp.asarray(table) for table in tables()])


def per_device(images, offsets, fractions, shifts):
    raw, par = exchange(images, offsets, fractions)
    return compute(shifts, raw, par)[None]


def solution(mesh):
    placed = (
        P("exp", None, "tile", None),
        P(None, "depth"),
        P(None, "depth"),
        P(("tile", "depth"), None),
    )
    return jax.shard_map(
        per_device,
        mesh=mesh,
        in_specs=placed,
        out_specs=P(("tile", "depth"), "exp", None),
        check_vma=False,
    )
```

time: 557 us -> 83 us (0.15)
  waiting for transfers between devices: 428 us -> 0 us
  Pallas kernels: 0 us -> 80.3 us
  matrix products: 36.3 us -> 0 us
  other arithmetic: 35.9 us -> 0 us
  local copies, waits for them, and re-layouts: 26.8 us -> 2.49 us
  between operations: 13.9 us -> 0.05 us
  starting transfers between devices: 12.8 us -> 0 us
    psum x2 -> x0, waiting for transfers between devices: 345 us -> none  [per_device(): totals = lax.psum(partial_value, 'depth')]
    pallas_call x0 -> x2, Pallas kernels: none -> 80.3 us  [the longest x1 61.9 us: compute(): pl.pallas_call(compute_kernel, out_shape=jax.ShapeDtypeStruct((BRICK // 2...]
    ppermute x9 -> x0, waiting for transfers between devices: 52 us -> none  [the longest x1 45.6 us: partner_2(): return lax.ppermute(value, axis, pairs)]
    dot_general x12 -> x0, matrix products: 36.3 us -> none  [the longest x2 8.6 us: per_device(): jnp.dot(fwd_table, padded.reshape(slab * padded_width, rows_y), precision...]
    all_to_all x1 -> x0, waiting for transfers between devices: 30.7 us -> none  [per_device(): lax.all_to_all(blocks, 'depth', split_axis=0, concat_axis=1, tiled=True)]
    select_n x3 -> x0, other arithmetic: 24.5 us -> none  [the longest x1 11.9 us: cross_power(): out_re = jnp.where(anchor, 0.0, out_re)]
    reshape x5 -> x0, local copies, waits for them, and re-layouts: 19.4 us -> none  [the longest x2 16.2 us: per_device(): blocks = blocks.reshape(bricks_x * bricks_y, slab, brick * brick)]
    ppermute x9 -> x0, starting transfers between devices: 7.02 us -> none  [the longest x4 5.38 us: with_halo(): lax.ppermute(head, axis, [((i + 1) % count, i) for i in range(count)])]
  transfers between devices with their start and end apart: 12 -> 0, of which waited for: 8 -> 0; matrix products, arithmetic and copies ran while one was open for 1% -> 0% of each run, Pallas kernels for 0% -> 0%
where the time goes in v1:
time: 83 us; the launch traced here: 82.8 us
  Pallas kernels  80.3 us (97%)
  local copies, waits for them, and re-layouts  2.49 us (3%)
    pallas_call x1, Pallas kernels, compute(): pl.pallas_call(compute_kernel, out_shape=jax.ShapeDtypeStruct((BRICK // 2...  61.9 us
    pallas_call x1, Pallas kernels, exchange(): pl.pallas_call(exchange_kernel, out_shape=[jax.ShapeDtypeStruct((2, 4, CO...  18.3 us
    unnamed x12, local copies, waits for them, and re-layouts  2.49 us

profile of v1, /device:TPU:2, one launch (start us, length us, event | category | flops | bytes accessed | tf_op | source)
XLA Modules:
  0.0 82.8 jit_solution(18152797013720357388)
XLA Ops:
  0.0 0.0 copy-start.1
  0.0 0.0 copy-start.2
  0.0 0.0 copy-start.4
  0.0 18.3 %shard_map.73 = (f32[2,4,112,128]{3,2,1,0:T(8,128)}, f32[16,8,128]{2,1,0:T(8,128)}) custom-call(s32[4,4]{1,0:T(4,128)} %off_ref.1, f32[4,4]{1,0:T(4,128)} %frac_ref.1, f32[1,4,128,512]{3,2,1,0:T(8,128)} %img_ref.1), custom_call_target="tpu_custom_call" | custom-call | tf_op jit(solution)/shard_map/pallas_call | solution.py:118
  18.4 0.0 copy-start.5
  18.4 0.0 copy-done.1
  18.4 0.0 copy-done.2
  18.4 0.0 copy-done.4
  18.4 0.6 copy-done.5
  19.0 0.0 copy-start
  19.0 1.0 %copy-done = f32[2,4,112,128]{3,2,1,0:T(8,128)S(1)} copy-done((f32[2,4,112,128]{3,2,1,0:T(8,128)S(1)}, f32[2,4,112,128]{3,2,1,0:T(8,128)}, u32[]{:S(2)}) %copy-start) | copy-done | bytes 458776
  20.0 0.0 copy-start.3
  20.0 0.8 %copy-done.3 = f32[16,8,128]{2,1,0:T(8,128)S(1)} copy-done((f32[16,8,128]{2,1,0:T(8,128)S(1)}, f32[16,8,128]{2,1,0:T(8,128)}, u32[]{:S(2)}) %copy-start.3) | copy-done | bytes 65560
  20.9 61.9 %shard_map.74 = f32[32,4096]{1,0:T(8,128)} custom-call(s32[1,3]{1,0:T(1,128)S(1)} %copy-done.5, f32[2,4,112,128]{3,2,1,0:T(8,128)S(1)} %copy-done, f32[16,8,128]{2,1,0:T(8,128)S(1)} %copy-done.3, bf16[64,192]{1,0:T(8,128)(2,1)S(1)} %copy-done.4, bf16[768,256]{1,0:T(8,128)(2,1)S(1)} %copy-done.1, bf16[128,192]{1,0:T(8,128)(2,1)S(1)} %copy-done.2), custom_call_target="tpu_custom_call" | custom-call | tf_op jit(solution)/shard_map/pallas_call | solution.py:376
Async XLA Ops:
  0.0 18.4 %copy-start.1 = (bf16[768,256]{1,0:T(8,128)(2,1)S(1)}, bf16[768,256]{1,0:T(8,128)(2,1)}, u32[]{:S(2)}) copy-start(bf16[768,256]{1,0:T(8,128)(2,1)} %constant.7.clone.ty_ref) | copy-start | bytes 1179652
  0.0 18.4 %copy-start.2 = (bf16[128,192]{1,0:T(8,128)(2,1)S(1)}, bf16[128,192]{1,0:T(8,128)(2,1)}, u32[]{:S(2)}) copy-start(bf16[128,192]{1,0:T(8,128)(2,1)} %constant.8.clone.cs_ref) | copy-start | bytes 147460
  0.0 18.4 %copy-start.4 = (bf16[64,192]{1,0:T(8,128)(2,1)S(1)}, bf16[64,192]{1,0:T(8,128)(2,1)}, u32[]{:S(2)}) copy-start(bf16[64,192]{1,0:T(8,128)(2,1)} %constant.6.clone.fz_ref) | copy-start | bytes 73732
  18.4 0.7 copy-start.5
  19.0 1.0 %copy-start = (f32[2,4,112,128]{3,2,1,0:T(8,128)S(1)}, f32[2,4,112,128]{3,2,1,0:T(8,128)}, u32[]{:S(2)}) copy-start(f32[2,4,112,128]{3,2,1,0:T(8,128)} %get-tuple-element.7.raw_ref) | copy-start | bytes 1376260
  20.0 0.8 %copy-start.3 = (f32[16,8,128]{2,1,0:T(8,128)S(1)}, f32[16,8,128]{2,1,0:T(8,128)}, u32[]{:S(2)}) copy-start(f32[16,8,128]{2,1,0:T(8,128)} %get-tuple-element.8.par_ref) | copy-start | bytes 196612

commit v2 on v1

--- a/solution.py
+++ b/solution.py
@@ -20,6 +20,7 @@
 MAIN = BRICK + EDGE
 PEERS = 16
 FLOOR = 0.01
+UN2, UN3, UN4, PB = 48, 32, 16, 33
 F32 = jnp.float32
 BF16 = jnp.bfloat16
 
@@ -243,12 +244,13 @@
         return jnp.concatenate(high + of(low_ref) + high, axis=0)
 
     def second(i, carry):
-        x = 2 * i
-        volume = jnp.exp(dot(back, windows(rh, rl, x)))
-        g[:, pl.ds(pl.multiple_of(x * LANES, LANES), 2 * LANES)] = dot(forward, stack_rows(volume))
+        for k in range(UN2):
+            x = 2 * (UN2 * i + k)
+            volume = jnp.exp(dot(back, windows(rh, rl, x)))
+            g[:, pl.ds(pl.multiple_of(x * LANES, LANES), 2 * LANES)] = dot(forward, stack_rows(volume))
         return carry
 
-    lax.fori_loop(0, COLS_V // 2, second, 0)
+    lax.fori_loop(0, COLS_V // 2 // UN2, second, 0)
 
     chunk = 8
     for u in range(0, COLS_U, chunk):
@@ -285,15 +287,16 @@
     fz = fz_ref[...]
 
     def third(i, carry):
-        x = 2 * i
-        volume = jnp.exp(dot(back, windows(uh, ul, x)))
-        spec = dot(fz, stack_rows(volume))
-        start = pl.multiple_of(x * BRICK, BRICK)
-        zs[pl.ds(start, BRICK), :] = spec[:, :LANES]
-        zs[pl.ds(start + BRICK, BRICK), :] = spec[:, LANES:]
+        for k in range(UN3):
+            x = 2 * (UN3 * i + k)
+            volume = jnp.exp(dot(back, windows(uh, ul, x)))
+            spec = dot(fz, stack_rows(volume))
+            start = pl.multiple_of(x * BRICK, BRICK)
+            zs[pl.ds(start, BRICK), :] = spec[:, :LANES]
+            zs[pl.ds(start + BRICK, BRICK), :] = spec[:, LANES:]
         return carry
 
-    lax.fori_loop(0, BRICK // 2, third, 0)
+    lax.fori_loop(0, BRICK // 2 // UN3, third, 0)
 
     ty = ty_ref[...]
     cs = cs_ref[...]
@@ -302,13 +305,13 @@
     sign = jnp.where(low_half, -1.0, 1.0)
     row_zero = (iota((BRICK, LANES), 0) == 0) & (iota((BRICK, LANES), 1) % BRICK == 0)
 
-    def plane(kz):
+    def load_plane(kz):
         inner = (kz > 0) & (kz < 32)
-        im_row = jnp.where(inner, 32 + kz, kz)
         re = zs[pl.ds(kz, BRICK, stride=BRICK), :]
-        im = zs[pl.ds(im_row, BRICK, stride=BRICK), :]
-        im = jnp.where(inner, im, 0.0)
-        spec = dot(stack_lanes(jnp.concatenate([re, im], axis=1)), ty)
+        im = zs[pl.ds(jnp.where(inner, 32 + kz, kz), BRICK, stride=BRICK), :]
+        return jnp.concatenate([re, jnp.where(inner, im, 0.0)], axis=1)
+
+    def cross_of(spec, kz):
         spec = dot(cs, stack_rows(spec))
         s_re = spec[:BRICK, :LANES] + spec[BRICK:, LANES:]
         s_im = spec[:BRICK, LANES:] - spec[BRICK:, :LANES]
@@ -318,35 +321,41 @@
             lax.rsqrt((s_re * s_re + s_im * s_im) * (m_re * m_re + m_im * m_im)), 1.0 / FLOOR
         )
         prod = jnp.where(low_half, s_re * m_re + s_im * m_im, s_im * m_re - s_re * m_im)
-        cross = jnp.where(row_zero & (kz == 0), 0.0, prod * inv)
-        back_y = dot(stack_lanes(cross), tiy)
+        return jnp.where(row_zero & (kz == 0), 0.0, prod * inv)
+
+    def store_plane(back_y, kz):
+        inner = (kz > 0) & (kz < 32)
         back_x = dot(tix, stack_rows(back_y))
         corr = back_x[:BRICK] + sign * pltpu.roll(back_x[BRICK:], BRICK, 1)
         even, odd_x = corr[: BRICK // 2], corr[BRICK // 2 :]
         qs[pl.ds(kz, BRICK // 2, stride=BRICK), :] = jnp.where(
             low_quarter, even, pltpu.roll(odd_x, BRICK, 1)
         )
-
-        @pl.when(inner)
-        def _():
-            qs[pl.ds(im_row, BRICK // 2, stride=BRICK), :] = jnp.where(
-                low_quarter, pltpu.roll(even, BRICK, 1), odd_x
-            )
+        im_row = jnp.where(inner, 32 + kz, BRICK * BRICK // 2)
+        qs[pl.ds(im_row, BRICK // 2, stride=BRICK), :] = jnp.where(
+            low_quarter, pltpu.roll(even, BRICK, 1), odd_x
+        )
 
     def planes(i, carry):
-        for k in range(3):
-            plane(3 * i + k)
+        ids = [PB * i + k for k in range(PB)]
+        spec = dot(stack_lanes(jnp.concatenate([load_plane(kz) for kz in ids], axis=0)), ty)
+        cross = [cross_of(spec[BRICK * k : BRICK * (k + 1)], kz) for k, kz in enumerate(ids)]
+        back_y = dot(stack_lanes(jnp.concatenate(cross, axis=0)), tiy)
+        for k, kz in enumerate(ids):
+            store_plane(back_y[BRICK * k : BRICK * (k + 1)], kz)
         return carry
 
-    lax.fori_loop(0, 11, planes, 0)
+    lax.fori_loop(0, 33 // PB, planes, 0)
 
     def last(i, carry):
-        start = pl.multiple_of(2 * i * BRICK, BRICK)
-        data = jnp.concatenate([qs[pl.ds(start, BRICK), :], qs[pl.ds(start + BRICK, BRICK), :]], axis=1)
-        out_ref[:, pl.ds(pl.multiple_of(2 * i * LANES, LANES), 2 * LANES)] = dot(tiz, stack_rows(data))
+        for k in range(UN4):
+            x = UN4 * i + k
+            start = pl.multiple_of(2 * x * BRICK, BRICK)
+            data = jnp.concatenate([qs[pl.ds(start, BRICK), :], qs[pl.ds(start + BRICK, BRICK), :]], axis=1)
+            out_ref[:, pl.ds(pl.multiple_of(2 * x * LANES, LANES), 2 * LANES)] = dot(tiz, stack_rows(data))
         return carry
 
-    lax.fori_loop(0, BRICK // 4, last, 0)
+    lax.fori_loop(0, BRICK // 4 // UN4, last, 0)
 
 
 def halves(table):
@@ -387,7 +396,7 @@
             pltpu.VMEM((16, COLS_U * LANES), BF16),
             pltpu.VMEM((16, COLS_U * LANES), BF16),
             pltpu.VMEM((BRICK * BRICK, LANES), F32),
-            pltpu.VMEM((BRICK * BRICK // 2, LANES), F32),
+            pltpu.VMEM((BRICK * BRICK, LANES), F32),
         ],
         compiler_params=pltpu.CompilerParams(vmem_limit_bytes=40 * 1024 * 1024),
     )(shifts, raw, par, *[jnp.asarray(table) for table in tables()])

time: 83 us -> 32.1 us (0.39)
  Pallas kernels: 80.3 us -> 29.4 us
    pallas_call x1, Pallas kernels: 61.9 us -> 11.1 us  [compute(): pl.pallas_call(compute_kernel, out_shape=jax.ShapeDtypeStruct((BRICK // 2...]
where the time goes in v2:
time: 32.1 us; the launch traced here: 31.9 us
  Pallas kernels  29.4 us (92%)
  local copies, waits for them, and re-layouts  2.49 us (8%)
    pallas_call x1, Pallas kernels, exchange(): pl.pallas_call(exchange_kernel, out_shape=[jax.ShapeDtypeStruct((2, 4, CO...  18.3 us
    pallas_call x1, Pallas kernels, compute(): pl.pallas_call(compute_kernel, out_shape=jax.ShapeDtypeStruct((BRICK // 2...  11.1 us
    unnamed x12, local copies, waits for them, and re-layouts  2.49 us

profile of v2, /device:TPU:2, one launch (start us, length us, event | category | flops | bytes accessed | tf_op | source)
XLA Modules:
  0.0 31.9 jit_solution(2875281184916436127)
XLA Ops:
  0.0 0.0 copy-start.1
  0.0 0.0 copy-start.2
  0.0 0.0 copy-start.4
  0.0 18.3 %shard_map.73 = (f32[2,4,112,128]{3,2,1,0:T(8,128)}, f32[16,8,128]{2,1,0:T(8,128)}) custom-call(s32[4,4]{1,0:T(4,128)} %off_ref.1, f32[4,4]{1,0:T(4,128)} %frac_ref.1, f32[1,4,128,512]{3,2,1,0:T(8,128)} %img_ref.1), custom_call_target="tpu_custom_call" | custom-call | tf_op jit(solution)/shard_map/pallas_call | solution.py:119
  18.4 0.0 copy-start.5
  18.4 0.0 copy-done.1
  18.4 0.0 copy-done.2
  18.4 0.0 copy-done.4
  18.4 0.6 %copy-done.5 = s32[1,3]{1,0:T(1,128)S(1)} copy-done((s32[1,3]{1,0:T(1,128)S(1)}, s32[1,3]{1,0:T(1,128)}, u32[]{:S(2)}) %copy-start.5) | copy-done | bytes 36
  19.0 0.0 copy-start
  19.0 1.0 %copy-done = f32[2,4,112,128]{3,2,1,0:T(8,128)S(1)} copy-done((f32[2,4,112,128]{3,2,1,0:T(8,128)S(1)}, f32[2,4,112,128]{3,2,1,0:T(8,128)}, u32[]{:S(2)}) %copy-start) | copy-done | bytes 458776
  20.0 0.0 copy-start.3
  20.0 0.8 %copy-done.3 = f32[16,8,128]{2,1,0:T(8,128)S(1)} copy-done((f32[16,8,128]{2,1,0:T(8,128)S(1)}, f32[16,8,128]{2,1,0:T(8,128)}, u32[]{:S(2)}) %copy-start.3) | copy-done | bytes 65560
  20.9 11.1 %shard_map.74 = f32[32,4096]{1,0:T(8,128)} custom-call(s32[1,3]{1,0:T(1,128)S(1)} %copy-done.5, f32[2,4,112,128]{3,2,1,0:T(8,128)S(1)} %copy-done, f32[16,8,128]{2,1,0:T(8,128)S(1)} %copy-done.3, bf16[64,192]{1,0:T(8,128)(2,1)S(1)} %copy-done.4, bf16[768,256]{1,0:T(8,128)(2,1)S(1)} %copy-done.1, bf16[128,192]{1,0:T(8,128)(2,1)S(1)} %copy-done.2), custom_call_target="tpu_custom_call" | custom-call | tf_op jit(solution)/shard_map/pallas_call | solution.py:385
Async XLA Ops:
  0.0 18.4 %copy-start.1 = (bf16[768,256]{1,0:T(8,128)(2,1)S(1)}, bf16[768,256]{1,0:T(8,128)(2,1)}, u32[]{:S(2)}) copy-start(bf16[768,256]{1,0:T(8,128)(2,1)} %constant.7.clone.ty_ref) | copy-start | bytes 1179652
  0.0 18.4 %copy-start.2 = (bf16[128,192]{1,0:T(8,128)(2,1)S(1)}, bf16[128,192]{1,0:T(8,128)(2,1)}, u32[]{:S(2)}) copy-start(bf16[128,192]{1,0:T(8,128)(2,1)} %constant.8.clone.cs_ref) | copy-start | bytes 147460
  0.0 18.4 %copy-start.4 = (bf16[64,192]{1,0:T(8,128)(2,1)S(1)}, bf16[64,192]{1,0:T(8,128)(2,1)}, u32[]{:S(2)}) copy-start(bf16[64,192]{1,0:T(8,128)(2,1)} %constant.6.clone.fz_ref) | copy-start | bytes 73732
  18.4 0.7 %copy-start.5 = (s32[1,3]{1,0:T(1,128)S(1)}, s32[1,3]{1,0:T(1,128)}, u32[]{:S(2)}) copy-start(s32[1,3]{1,0:T(1,128)} %shift_ref.1) | copy-start | bytes 40
  19.0 1.0 %copy-start = (f32[2,4,112,128]{3,2,1,0:T(8,128)S(1)}, f32[2,4,112,128]{3,2,1,0:T(8,128)}, u32[]{:S(2)}) copy-start(f32[2,4,112,128]{3,2,1,0:T(8,128)} %get-tuple-element.7.raw_ref) | copy-start | bytes 1376260
  20.0 0.8 %copy-start.3 = (f32[16,8,128]{2,1,0:T(8,128)S(1)}, f32[16,8,128]{2,1,0:T(8,128)}, u32[]{:S(2)}) copy-start(f32[16,8,128]{2,1,0:T(8,128)} %get-tuple-element.8.par_ref) | copy-start | bytes 196612

commit v3 on v1

v3 whole, which is shorter than its diff:
```python
import functools
import math

import jax
import jax.numpy as jnp
import ml_dtypes
import numpy as np
from jax import lax
from jax.experimental import pallas as pl
from jax.experimental.pallas import tpu as pltpu
from jax.sharding import PartitionSpec as P

MESH = pl.DeviceIdType.MESH
BRICK = 64
LANES = 128
EDGE = 24
COLS_R = BRICK + 2 * EDGE
COLS_V = BRICK + 32
COLS_U = BRICK + 16
MAIN = BRICK + EDGE
PEERS = 16
FLOOR = 0.01
F32 = jnp.float32
BF16 = jnp.bfloat16
VMEM_LIMIT = 60 * 1024 * 1024
HANDED = [
    ((PEERS, 8, LANES), F32),
    ((8 * COLS_R, LANES), F32),
    ((16, COLS_R * LANES), BF16),
    ((16, COLS_R * LANES), BF16),
    ((2 * BRICK, 3 * BRICK), BF16),
    ((4 * BRICK, 2 * LANES), BF16),
    ((BRICK // 2, 3 * BRICK), BF16),
]
TABLES = [((BRICK, 3 * BRICK), BF16), ((12 * BRICK, 4 * BRICK), BF16), ((2 * BRICK, 3 * BRICK), BF16)]


def split(value):
    high = value.astype(BF16)
    low = (value - high.astype(F32)).astype(BF16)
    return high, low


def stack_rows(value):
    high, low = split(value)
    return jnp.concatenate([high, low, high], axis=0)


def stack_lanes(value):
    high, low = split(value)
    return jnp.concatenate([high, low, high], axis=1)


def twice(value):
    high, low = split(value)
    return jnp.concatenate([high, low[:, :BRICK]], axis=1)


def dot(left, right):
    return jnp.dot(left, right, preferred_element_type=F32)


def turn_cos(turns):
    return jnp.cos((turns & (BRICK - 1)).astype(F32) * (2.0 * math.pi / BRICK)) * 0.125


def iota(shape, axis):
    return lax.broadcasted_iota(jnp.int32, shape, axis)


def exchange_kernel(
    off_hbm, frac_hbm, shift_hbm, img_ref, par_out, r8_out, rh_out, rl_out, tix_out, tiy_out, tiz_out,
    off_ref, frac_ref, shift_ref, stage, stage_far, own, far, packed,
    par_ref, r8, rh, rl, tix_ref, tiy_ref, tiz_ref, local, out_sem, z_send, z_recv, y_send, y_recv, i_send, i_recv,
):
    e = lax.axis_index("exp")
    t = lax.axis_index("tile")
    d = lax.axis_index("depth")
    tiles = lax.axis_size("tile")
    other = 1 - e
    yy, zh = d // 4, lax.rem(d, 4)
    half = d // 8
    side = 2 * e - 1

    def depth_of(y, z):
        return lax.rem(y, 4) * 4 + lax.rem(z + 4, 4)

    d_far = depth_of(yy, zh + side)
    t_to = lax.rem(t + 1 - 2 * half + tiles, tiles)
    t_from = lax.rem(t - 1 + 2 * half + tiles, tiles)
    z_to = [(other, t, d_far), (e, t, d_far), (other, t, depth_of(yy, zh + 2))]
    y_to = [(e, t, depth_of(yy + k, zh)) for k in range(1, 4)]
    sources = [(other, t, d_far), (e, t, depth_of(yy, zh - side)), (other, t, depth_of(yy, zh + 2))]
    sources += y_to + [(other, t, d), (e, t_from, d), (other, t_from, d)]

    barrier = pltpu.get_barrier_semaphore()
    for source in sources:
        pl.semaphore_signal(barrier, inc=1, device_id=source, device_id_type=MESH)

    def lanes_of(depth):
        return pl.ds(pl.multiple_of(lax.rem(depth, 8) // 2 * LANES, LANES), LANES)

    main_src = pl.ds(pl.multiple_of((BRICK - EDGE) * half, 8), MAIN)
    main_dst = pl.ds(pl.multiple_of(EDGE * (1 - half), 8), MAIN)
    strip_src = pl.ds(pl.multiple_of((2 * BRICK - EDGE) * (1 - half), 8), EDGE)
    strip_dst = pl.ds(pl.multiple_of(MAIN * half, 8), EDGE)

    small = [
        pltpu.make_async_copy(off_hbm, off_ref, local.at[0]),
        pltpu.make_async_copy(frac_hbm, frac_ref, local.at[1]),
        pltpu.make_async_copy(shift_hbm, shift_ref, local.at[2]),
    ]
    large = [
        pltpu.make_async_copy(img_ref.at[0, :, :, lanes_of(d)], stage, local.at[3]),
        pltpu.make_async_copy(img_ref.at[0, pl.ds(2, 2), main_src, lanes_of(d_far)], stage_far, local.at[4]),
    ]
    for copy in small + large:
        copy.start()
    small[0].wait()
    small[1].wait()

    row = iota((8, LANES), 0)
    cam = iota((8, LANES), 1) % 4
    tile = jnp.zeros((8, LANES), F32)
    for c in range(4):
        for z in range(4):
            tile = jnp.where((row == z) & (cam == c), off_ref[c, z].astype(F32), tile)
            tile = jnp.where((row == z + 4) & (cam == c), frac_ref[c, z], tile)
    par_ref[d] = tile

    def remote(source, target, sends, recvs, index, device):
        return pltpu.make_async_remote_copy(
            src_ref=source,
            dst_ref=target,
            send_sem=sends.at[index],
            recv_sem=recvs.at[index],
            device_id=device,
            device_id_type=MESH,
        )

    along_z = [remote(par_ref.at[d], par_ref.at[d], z_send, z_recv, k, to) for k, to in enumerate(z_to)]
    rows = pl.ds(pl.multiple_of(4 * yy, 4), 4)
    along_y = [remote(par_ref.at[rows], par_ref.at[rows], y_send, y_recv, k, to) for k, to in enumerate(y_to)]
    pixels = [
        remote(own.at[:, strip_src, :], packed.at[e, :, strip_dst, :], i_send, i_recv, 0, (e, t_to, d)),
        remote(own.at[:, strip_src, :], packed.at[e, :, strip_dst, :], i_send, i_recv, 1, (other, t_to, d)),
        remote(own.at[0, main_src, :], packed.at[e, 0, main_dst, :], i_send, i_recv, 2, (other, t, d)),
        remote(far, packed.at[e, 1, main_dst, :], i_send, i_recv, 3, (other, t, d_far)),
    ]

    pl.semaphore_wait(barrier, len(sources))
    for copy in along_z:
        copy.start()

    def pack(even, odd, high_half):
        low = iota(even.shape, 1) < BRICK
        kept = jnp.where(high_half, odd, even)
        moved = pltpu.roll(jnp.where(high_half, even, odd), BRICK, 1)
        return jnp.log(jnp.where(low != high_half, kept, moved))

    for copy in large:
        copy.wait()
    for pair in range(2):
        own[pair] = pack(stage[2 * pair], stage[2 * pair + 1], lax.rem(d, 2) == 1)
    far[...] = pack(stage_far[0], stage_far[1], lax.rem(d_far, 2) == 1)
    for copy in pixels:
        copy.start()
    packed[e, :, main_dst, :] = own[:, main_src, :]

    small[2].wait()
    sz, sx, sy = shift_ref[0, 0], shift_ref[0, 1], shift_ref[0, 2]
    r = iota((2 * BRICK, LANES), 0)
    c = iota((2 * BRICK, LANES), 1)
    y_high, y_low = split(turn_cos((r % BRICK) * (c % BRICK + sy) + 16 * (r // BRICK - c // BRICK)))
    zero = jnp.zeros_like(y_low)
    tiy_ref[...] = jnp.concatenate(
        [jnp.concatenate([y_high, y_low], axis=1), jnp.concatenate([y_high, zero], axis=1)], axis=0
    )
    x_of = 2 * (r % (BRICK // 2)) + (r % BRICK) // (BRICK // 2)
    tix_ref[...] = twice(turn_cos((c % BRICK) * (x_of + sx) - 16 * (r // BRICK)))
    r = iota((BRICK // 2, LANES), 0)
    c = iota((BRICK // 2, LANES), 1) % BRICK
    kz = jnp.where(c > 32, c - 32, c)
    weight = jnp.where((kz == 0) | (kz == 32), 1.0, 2.0)
    tiz_ref[...] = twice(weight * turn_cos(kz * (r + 32 * e + sz) + jnp.where(c > 32, 16, 0)))

    results = [
        pltpu.make_async_copy(source, target, out_sem.at[k])
        for k, (source, target) in enumerate(
            [(tix_ref, tix_out), (tiy_ref, tiy_out), (tiz_ref, tiz_out), (r8, r8_out), (rh, rh_out), (rl, rl_out), (par_ref, par_out)]
        )
    ]
    for copy in results[:3]:
        copy.start()

    for copy in along_z:
        copy.wait_recv()
    for copy in along_y:
        copy.start()
    for copy in pixels:
        copy.wait_recv()

    low = iota((COLS_R, LANES), 1) < BRICK
    for pair in range(2):
        one, two = packed[0, pair], packed[1, pair]
        both = [
            jnp.where(low, one, pltpu.roll(two, BRICK, 1)),
            jnp.where(low, pltpu.roll(one, BRICK, 1), two),
        ]
        for k in range(2):
            c = 2 * pair + k
            r8[c * COLS_R : (c + 1) * COLS_R, :] = both[k]
            r8[(c + 4) * COLS_R : (c + 5) * COLS_R, :] = pltpu.roll(both[k], COLS_R - 1, 0)
    for x in range(COLS_R - 2):
        col = jnp.concatenate(
            [r8[pl.ds(x, 8, stride=COLS_R), :], r8[pl.ds(x + 2, 8, stride=COLS_R), :]], axis=0
        )
        high, lows = split(col)
        rh[:, x * LANES : (x + 1) * LANES] = high
        rl[:, x * LANES : (x + 1) * LANES] = lows

    for copy in results[3:6]:
        copy.start()
    for copy in along_y:
        copy.wait_recv()
    results[6].start()
    for copy in along_z + along_y + pixels:
        copy.wait_send()
    for copy in results:
        copy.wait()


def exchange(images, offsets, fractions, shifts):
    hbm = pl.BlockSpec(memory_space=pltpu.HBM)
    return pl.pallas_call(
        exchange_kernel,
        out_shape=[jax.ShapeDtypeStruct(shape, dtype) for shape, dtype in HANDED],
        in_specs=[hbm] * 4,
        out_specs=[hbm] * 7,
        scratch_shapes=[
            pltpu.SMEM((4, 4), jnp.int32),
            pltpu.SMEM((4, 4), F32),
            pltpu.SMEM((1, 3), jnp.int32),
            pltpu.VMEM((4, 2 * BRICK, LANES), F32),
            pltpu.VMEM((2, MAIN, LANES), F32),
            pltpu.VMEM((2, 2 * BRICK, LANES), F32),
            pltpu.VMEM((MAIN, LANES), F32),
            pltpu.VMEM((2, 2, COLS_R, LANES), F32),
            *[pltpu.VMEM(shape, dtype) for shape, dtype in HANDED],
            pltpu.SemaphoreType.DMA((5,)),
            pltpu.SemaphoreType.DMA((len(HANDED),)),
            pltpu.SemaphoreType.DMA((3,)),
            pltpu.SemaphoreType.DMA((3,)),
            pltpu.SemaphoreType.DMA((3,)),
            pltpu.SemaphoreType.DMA((3,)),
            pltpu.SemaphoreType.DMA((4,)),
            pltpu.SemaphoreType.DMA((4,)),
        ],
        compiler_params=pltpu.CompilerParams(
            collective_id=0, has_side_effects=True, vmem_limit_bytes=VMEM_LIMIT
        ),
    )(offsets, fractions, shifts, images)


def compute_kernel(
    *refs
):
    count = len(HANDED + TABLES)
    out_ref = refs[count]
    g, a8, uh, ul, zs, qs, result, done, loaded = refs[2 * count + 1 :]
    loads = [
        pltpu.make_async_copy(refs[k], refs[count + 1 + k], loaded.at[k]) for k in range(count)
    ]
    order = (0, 2, 3, 1, 7, 8, 9, 4, 5, 6)
    for k in order:
        loads[k].start()
    par_ref, r8, rh, rl, tix_ref, tiy_ref, tiz_ref, fz_ref, ty_ref, cs_ref = refs[count + 1 : 2 * count + 1]
    loads[0].wait()

    sub = iota((8, LANES), 0)
    offs, fracs = [], []
    for i in range(PEERS // 2):
        a, b = par_ref[2 * i], par_ref[2 * i + 1]
        offs.append(jnp.where(sub < 4, a, pltpu.roll(b, 4, 0)))
        fracs.append(jnp.where(sub < 4, pltpu.roll(a, 4, 0), b))
    off = jnp.concatenate(offs, axis=0)
    frac = jnp.concatenate(fracs, axis=0)
    s_of = iota((BRICK, LANES), 1) % BRICK // 4 - 7

    def tent(distance):
        return jnp.maximum(0.0, 1.0 - jnp.abs(distance - frac) / 1.5)

    total = tent(-2.0)
    for tap in range(-1, 4):
        total = total + tent(float(tap))
    weights = tent(s_of.astype(F32) - off) / total * 0.25
    back = twice(weights)
    turned = jnp.concatenate([weights, weights], axis=0).T[:BRICK] * 0.0625
    forward = twice(turned)
    ones = jnp.sum(turned[:, :BRICK], axis=1, keepdims=True)
    first = ones[0:8]
    for i in range(1, 8):
        first = first + ones[8 * i : 8 * i + 8]
    first = first + pltpu.roll(jnp.broadcast_to(first, (8, LANES)), 4, 0)
    log_first = jnp.log(first)
    by_lane = jnp.broadcast_to(jnp.sum(weights, axis=0, keepdims=True) * 0.0625, (8, LANES))
    for step in (4, 8, 16, 32):
        by_lane = by_lane + pltpu.roll(by_lane, step, 1)
    lift = jnp.sum(weights * jnp.log(by_lane[0:1]), axis=1, keepdims=True) * 0.5
    lift = jnp.broadcast_to(lift, (BRICK, 2 * LANES))

    for k in order[1:]:
        loads[k].wait()

    def windows(high_ref, low_ref, x):
        def of(ref):
            return [ref[:, (x + 1 + 4 * q) * LANES : (x + 3 + 4 * q) * LANES] for q in range(4)]

        high = of(high_ref)
        return jnp.concatenate(high + of(low_ref) + high, axis=0)

    for x in range(0, COLS_V, 2):
        volume = jnp.exp(dot(back, windows(rh, rl, x)) - lift)
        g[:, x * LANES : (x + 2) * LANES] = dot(forward, stack_rows(volume))

    chunk = 8
    for u in range(0, COLS_U, chunk):
        n = (chunk + 1) * LANES

        def group(row, shift):
            total = None
            for q in range(4):
                start = (u + shift + 12 - 4 * q) * LANES
                part = g[16 * q + row : 16 * q + row + 8, start : start + n]
                total = part if total is None else total + part
            return total

        pairs = group(0, 2) + group(8, 0)
        proj = pairs[:, LANES:] + pltpu.roll(pairs[:, : chunk * LANES], 4, 0)
        log_proj = jnp.log(proj)
        for i in range(chunk):
            ratio = r8[pl.ds(u + i + 16, 8, stride=COLS_R), :]
            a8[:, (u + i) * LANES : (u + i + 1) * LANES] = (
                2.0 * ratio - log_first - log_proj[:, i * LANES : (i + 1) * LANES]
            )

    def column(u):
        return a8[:, u * LANES : (u + 1) * LANES]

    def pair(u):
        return jnp.where(sub < 4, column(u), pltpu.roll(column(u + 1), 4, 0))

    for u in range(COLS_U - 3):
        high, low = split(jnp.concatenate([pair(u), pair(u + 2)], axis=0))
        uh[:, u * LANES : (u + 1) * LANES] = high
        ul[:, u * LANES : (u + 1) * LANES] = low

    fz = fz_ref[...]

    for x in range(0, BRICK, 2):
        volume = jnp.exp(dot(back, windows(uh, ul, x)))
        spec = dot(fz, stack_rows(volume))
        zs[x * BRICK : (x + 1) * BRICK, :] = spec[:, :LANES]
        zs[(x + 1) * BRICK : (x + 2) * BRICK, :] = spec[:, LANES:]

    ty = ty_ref[...]
    tix, tiy, tiz = tix_ref[...], tiy_ref[...], tiz_ref[...]
    cs = cs_ref[...]
    low_half = iota((BRICK, LANES), 1) < BRICK
    low_quarter = iota((BRICK // 2, LANES), 1) < BRICK
    sign = jnp.where(low_half, -1.0, 1.0)
    row_zero = (iota((BRICK, LANES), 0) == 0) & (iota((BRICK, LANES), 1) % BRICK == 0)

    def load_plane(kz):
        re = zs[pl.ds(kz, BRICK, stride=BRICK), :]
        if 0 < kz < 32:
            im = zs[pl.ds(32 + kz, BRICK, stride=BRICK), :]
        else:
            im = jnp.zeros_like(re)
        return jnp.concatenate([re, im], axis=1)

    def cross_of(spec, kz):
        spec = dot(cs, stack_rows(spec))
        s_re = spec[:BRICK, :LANES] + spec[BRICK:, LANES:]
        s_im = spec[:BRICK, LANES:] - spec[BRICK:, :LANES]
        m_re = pltpu.roll(s_re, BRICK, 1)
        m_im = pltpu.roll(s_im, BRICK, 1)
        inv = jnp.minimum(
            lax.rsqrt((s_re * s_re + s_im * s_im) * (m_re * m_re + m_im * m_im)), 1.0 / FLOOR
        )
        prod = jnp.where(low_half, s_re * m_re + s_im * m_im, s_im * m_re - s_re * m_im)
        cross = prod * inv
        return jnp.where(row_zero, 0.0, cross) if kz == 0 else cross

    def store_planes(back_y, ids):
        n = len(ids)
        back_x = dot(tix, stack_rows(jnp.concatenate(back_y, axis=1)))
        for k, kz in enumerate(ids):
            part = back_x[:, k * LANES : (k + 1) * LANES]
            corr = part[:BRICK] + sign * pltpu.roll(part[BRICK:], BRICK, 1)
            even, odd_x = corr[: BRICK // 2], corr[BRICK // 2 :]
            qs[pl.ds(kz, BRICK // 2, stride=BRICK), :] = jnp.where(
                low_quarter, even, pltpu.roll(odd_x, BRICK, 1)
            )
            if 0 < kz < 32:
                qs[pl.ds(32 + kz, BRICK // 2, stride=BRICK), :] = jnp.where(
                    low_quarter, pltpu.roll(even, BRICK, 1), odd_x
                )

    ids = range(BRICK // 2 + 1)
    spec = dot(stack_lanes(jnp.concatenate([load_plane(kz) for kz in ids], axis=0)), ty)
    cross = [cross_of(spec[BRICK * kz : BRICK * (kz + 1)], kz) for kz in ids]
    back_y = dot(jnp.concatenate(split(jnp.concatenate(cross, axis=0)), axis=1), tiy)
    back_y = back_y[:, :LANES] + back_y[:, LANES:]
    back_y = [back_y[BRICK * kz : BRICK * (kz + 1)] for kz in ids]
    for kz in range(0, len(ids), 2):
        store_planes(back_y[kz : kz + 2], ids[kz : kz + 2])

    copies = []
    for x in range(BRICK // 4):
        data = jnp.concatenate(
            [qs[BRICK * k : BRICK * (k + 1), :] for k in (2 * x, 2 * x + 1)], axis=1
        )
        result[:, 2 * x * LANES : 2 * (x + 1) * LANES] = dot(tiz, stack_rows(data))
        if x % 4 == 3:
            chunk = pl.ds((x // 4) * 8 * LANES, 8 * LANES)
            copies.append(pltpu.make_async_copy(result.at[:, chunk], out_ref.at[:, chunk], done.at[x // 4]))
            copies[-1].start()
    for copy in copies:
        copy.wait()


def halves(table):
    high = table.astype(ml_dtypes.bfloat16)
    low = (table - high.astype(np.float64)).astype(ml_dtypes.bfloat16)
    return high, low


@functools.cache
def tables():
    wave = np.arange(BRICK)
    angle = 2.0 * np.pi / BRICK * (wave[:, None] * wave[None, :] % BRICK)
    cos, sin = np.cos(angle) / 8.0, np.sin(angle) / 8.0
    high, low = halves(np.concatenate([cos[:33], -sin[1:32]], axis=0))
    fz = np.concatenate([high, high, low], axis=1)
    eye = np.eye(2)
    cos2, sin2 = np.kron(eye, cos), np.kron(eye, sin)
    high, low = halves(np.block([[cos2, -sin2], [sin2, cos2]]))
    ty = np.concatenate([high, high, low], axis=0)
    high, low = halves(np.concatenate([cos, sin], axis=0))
    cs = np.concatenate([high, high, low], axis=1)
    return fz, ty, cs


def compute(*exchanged):
    hbm = pl.BlockSpec(memory_space=pltpu.HBM)
    return pl.pallas_call(
        compute_kernel,
        out_shape=jax.ShapeDtypeStruct((BRICK // 2, BRICK * BRICK), F32),
        in_specs=[hbm] * len(HANDED + TABLES),
        out_specs=hbm,
        scratch_shapes=[
            *[pltpu.VMEM(shape, dtype) for shape, dtype in HANDED + TABLES],
            pltpu.VMEM((BRICK, COLS_V * LANES), F32),
            pltpu.VMEM((8, COLS_U * LANES), F32),
            pltpu.VMEM((16, COLS_U * LANES), BF16),
            pltpu.VMEM((16, COLS_U * LANES), BF16),
            pltpu.VMEM((BRICK * BRICK, LANES), F32),
            pltpu.VMEM((BRICK * BRICK // 2, LANES), F32),
            pltpu.VMEM((BRICK // 2, BRICK * BRICK), F32),
            pltpu.SemaphoreType.DMA((4,)),
            pltpu.SemaphoreType.DMA((len(HANDED + TABLES),)),
        ],
        compiler_params=pltpu.CompilerParams(vmem_limit_bytes=VMEM_LIMIT),
    )(*exchanged, *[jnp.asarray(table) for table in tables()])


def per_device(images, offsets, fractions, shifts):
    return compute(*exchange(images, offsets, fractions, shifts))[None]


def solution(mesh):
    placed = (
        P("exp", None, "tile", None),
        P(None, "depth"),
        P(None, "depth"),
        P(("tile", "depth"), None),
    )
    return jax.shard_map(
        per_device,
        mesh=mesh,
        in_specs=placed,
        out_specs=P(("tile", "depth"), "exp", None),
        check_vma=False,
    )
```

time: 83 us -> 26.9 us (0.32)
  Pallas kernels: 80.3 us -> 26.6 us
  local copies, waits for them, and re-layouts: 2.49 us -> 0 us
    pallas_call x1, Pallas kernels: 61.9 us -> 10.6 us  [compute(): pl.pallas_call(compute_kernel, out_shape=jax.ShapeDtypeStruct((BRICK // 2...]
    unnamed x12 -> x0, local copies, waits for them, and re-layouts: 2.49 us -> none
    pallas_call x1, Pallas kernels: 18.3 us -> 16 us  [exchange(): pl.pallas_call(exchange_kernel, out_shape=[jax.ShapeDtypeStruct(shape, dt...]
where the time goes in v3:
time: 26.9 us; the launch traced here: 26.6 us
  Pallas kernels  26.6 us (99%)
    pallas_call x1, Pallas kernels, exchange(): pl.pallas_call(exchange_kernel, out_shape=[jax.ShapeDtypeStruct(shape, dt...  16 us
    pallas_call x1, Pallas kernels, compute(): pl.pallas_call(compute_kernel, out_shape=jax.ShapeDtypeStruct((BRICK // 2...  10.6 us

profile of v3, /device:TPU:2, one launch (start us, length us, event | category | flops | bytes accessed | tf_op | source)
XLA Modules:
  0.0 26.6 jit_solution(17752754413599257237)
XLA Ops:
  0.0 16.0 %shard_map.73 = (f32[16,8,128]{2,1,0:T(8,128)}, f32[896,128]{1,0:T(8,128)}, bf16[16,14336]{1,0:T(8,128)(2,1)}, bf16[16,14336]{1,0:T(8,128)(2,1)}, bf16[128,192]{...) custom-call(s32[4,4]{1,0:T(4,128)} %off_hbm.1, f32[4,4]{1,0:T(4,128)} %frac_hbm.1, ...), custom_call_target="tpu_custom_call" | custom-call | tf_op jit(solution)/shard_map/pallas_call | solution.py:235
  16.0 10.6 %shard_map.74 = f32[32,4096]{1,0:T(8,128)} custom-call(f32[16,8,128]{2,1,0:T(8,128)} %get-tuple-element.12.refs_0_, f32[896,128]{1,0:T(8,128)} %get-tuple-element.13.refs_1_, bf16[16,14336]{1,0:T(8,128)(2,1)} %get-tuple-element.14.refs_2_, bf16[16,14336]{1,0:T(8,128)(2,1)} %get-tuple-element.15.refs_3_, bf16[128,192]{1,0:T(8,128)(2,1)} %get-tuple-element.16.refs_4_, ...), custom_call_target="tpu_custom_call" | custom-call | tf_op jit(solution)/shard_map/pallas_call | solution.py:457

commit v4 on v3

--- a/solution.py
+++ b/solution.py
@@ -71,7 +71,7 @@
 def exchange_kernel(
     off_hbm, frac_hbm, shift_hbm, img_ref, par_out, r8_out, rh_out, rl_out, tix_out, tiy_out, tiz_out,
     off_ref, frac_ref, shift_ref, stage, stage_far, own, far, packed,
-    par_ref, r8, rh, rl, tix_ref, tiy_ref, tiz_ref, local, out_sem, z_send, z_recv, y_send, y_recv, i_send, i_recv,
+    par_ref, r8, rh, rl, tix_ref, tiy_ref, tiz_ref, local, out_sem, p_send, p_recv, i_send, i_recv,
 ):
     e = lax.axis_index("exp")
     t = lax.axis_index("tile")
@@ -88,10 +88,9 @@
     d_far = depth_of(yy, zh + side)
     t_to = lax.rem(t + 1 - 2 * half + tiles, tiles)
     t_from = lax.rem(t - 1 + 2 * half + tiles, tiles)
-    z_to = [(other, t, d_far), (e, t, d_far), (other, t, depth_of(yy, zh + 2))]
-    y_to = [(e, t, depth_of(yy + k, zh)) for k in range(1, 4)]
-    sources = [(other, t, d_far), (e, t, depth_of(yy, zh - side)), (other, t, depth_of(yy, zh + 2))]
-    sources += y_to + [(other, t, d), (e, t_from, d), (other, t_from, d)]
+    outer, inner = (other, t, d_far), (other, t, d)
+    y_next, y_back = (e, t, depth_of(yy + 1, zh)), (e, t, depth_of(yy + 3, zh))
+    sources = [outer, inner, y_next, y_back, (e, t_from, d), (other, t_from, d)]
 
     barrier = pltpu.get_barrier_semaphore()
     for source in sources:
@@ -138,9 +137,20 @@
             device_id_type=MESH,
         )
 
-    along_z = [remote(par_ref.at[d], par_ref.at[d], z_send, z_recv, k, to) for k, to in enumerate(z_to)]
-    rows = pl.ds(pl.multiple_of(4 * yy, 4), 4)
-    along_y = [remote(par_ref.at[rows], par_ref.at[rows], y_send, y_recv, k, to) for k, to in enumerate(y_to)]
+    def slabs(first, count):
+        return par_ref.at[pl.ds(first, count)]
+
+    def pass_on(first, count, index, device):
+        return remote(slabs(first, count), slabs(first, count), p_send, p_recv, index, device)
+
+    d_near = depth_of(yy, zh - side)
+    own_out = pass_on(d, 1, 0, outer)
+    far_in = pass_on(d_far, 1, 1, inner)
+    near_out = pass_on(d_near, 1, 2, outer)
+    row_next = pass_on(pl.multiple_of(4 * yy, 4), 4, 3, y_next)
+    row_back = pass_on(pl.multiple_of(4 * yy, 4), 4, 4, y_back)
+    row_on = pass_on(pl.multiple_of(depth_of(yy + 3, 0), 4), 4, 5, y_next)
+    offers = [own_out, far_in, near_out, row_next, row_back, row_on]
     pixels = [
         remote(own.at[:, strip_src, :], packed.at[e, :, strip_dst, :], i_send, i_recv, 0, (e, t_to, d)),
         remote(own.at[:, strip_src, :], packed.at[e, :, strip_dst, :], i_send, i_recv, 1, (other, t_to, d)),
@@ -149,8 +159,7 @@
     ]
 
     pl.semaphore_wait(barrier, len(sources))
-    for copy in along_z:
-        copy.start()
+    own_out.start()
 
     def pack(even, odd, high_half):
         low = iota(even.shape, 1) < BRICK
@@ -165,6 +174,8 @@
     far[...] = pack(stage_far[0], stage_far[1], lax.rem(d_far, 2) == 1)
     for copy in pixels:
         copy.start()
+    own_out.wait_recv()
+    far_in.start()
     packed[e, :, main_dst, :] = own[:, main_src, :]
 
     small[2].wait()
@@ -193,10 +204,8 @@
     for copy in results[:3]:
         copy.start()
 
-    for copy in along_z:
-        copy.wait_recv()
-    for copy in along_y:
-        copy.start()
+    far_in.wait_recv()
+    near_out.start()
     for copy in pixels:
         copy.wait_recv()
 
@@ -219,12 +228,17 @@
         rh[:, x * LANES : (x + 1) * LANES] = high
         rl[:, x * LANES : (x + 1) * LANES] = lows
 
+    near_out.wait_recv()
+    row_next.start()
+    row_back.start()
     for copy in results[3:6]:
         copy.start()
-    for copy in along_y:
-        copy.wait_recv()
+    row_next.wait_recv()
+    row_on.start()
+    row_back.wait_recv()
+    row_on.wait_recv()
     results[6].start()
-    for copy in along_z + along_y + pixels:
+    for copy in offers + pixels:
         copy.wait_send()
     for copy in results:
         copy.wait()
@@ -249,10 +263,8 @@
             *[pltpu.VMEM(shape, dtype) for shape, dtype in HANDED],
             pltpu.SemaphoreType.DMA((5,)),
             pltpu.SemaphoreType.DMA((len(HANDED),)),
-            pltpu.SemaphoreType.DMA((3,)),
-            pltpu.SemaphoreType.DMA((3,)),
-            pltpu.SemaphoreType.DMA((3,)),
-            pltpu.SemaphoreType.DMA((3,)),
+            pltpu.SemaphoreType.DMA((6,)),
+            pltpu.SemaphoreType.DMA((6,)),
             pltpu.SemaphoreType.DMA((4,)),
             pltpu.SemaphoreType.DMA((4,)),
         ],

time: 26.9 us -> 33.8 us (1.26)
  the two profiles are of different devices: /device:TPU:2 before, /device:TPU:8 now
where the time goes in v4:
time: 33.8 us; the launch traced here: 33.7 us
  Pallas kernels  33.7 us (100%)
    pallas_call x1, Pallas kernels, exchange(): pl.pallas_call(exchange_kernel, out_shape=[jax.ShapeDtypeStruct(shape, dt...  23.1 us
    pallas_call x1, Pallas kernels, compute(): pl.pallas_call(compute_kernel, out_shape=jax.ShapeDtypeStruct((BRICK // 2...  10.6 us

profile of v4, /device:TPU:8, one launch (start us, length us, event | category | flops | bytes accessed | tf_op | source)
XLA Modules:
  0.0 33.7 jit_solution(11228539531346871882)
XLA Ops:
  0.0 23.1 %shard_map.73 = (f32[16,8,128]{2,1,0:T(8,128)}, f32[896,128]{1,0:T(8,128)}, bf16[16,14336]{1,0:T(8,128)(2,1)}, bf16[16,14336]{1,0:T(8,128)(2,1)}, bf16[128,192]{...) custom-call(s32[4,4]{1,0:T(4,128)} %off_hbm.1, f32[4,4]{1,0:T(4,128)} %frac_hbm.1, ...), custom_call_target="tpu_custom_call" | custom-call | tf_op jit(solution)/shard_map/pallas_call | solution.py:249
  23.1 10.6 %shard_map.74 = f32[32,4096]{1,0:T(8,128)} custom-call(f32[16,8,128]{2,1,0:T(8,128)} %get-tuple-element.12.refs_0_, f32[896,128]{1,0:T(8,128)} %get-tuple-element.13.refs_1_, bf16[16,14336]{1,0:T(8,128)(2,1)} %get-tuple-element.14.refs_2_, bf16[16,14336]{1,0:T(8,128)(2,1)} %get-tuple-element.15.refs_3_, bf16[128,192]{1,0:T(8,128)(2,1)} %get-tuple-element.16.refs_4_, ...), custom_call_target="tpu_custom_call" | custom-call | tf_op jit(solution)/shard_map/pallas_call | solution.py:469

commit v5 on v3

--- a/solution.py
+++ b/solution.py
@@ -20,6 +20,7 @@
 MAIN = BRICK + EDGE
 PEERS = 16
 FLOOR = 0.01
+STEP = 72
 F32 = jnp.float32
 BF16 = jnp.bfloat16
 VMEM_LIMIT = 60 * 1024 * 1024
@@ -71,7 +72,7 @@
 def exchange_kernel(
     off_hbm, frac_hbm, shift_hbm, img_ref, par_out, r8_out, rh_out, rl_out, tix_out, tiy_out, tiz_out,
     off_ref, frac_ref, shift_ref, stage, stage_far, own, far, packed,
-    par_ref, r8, rh, rl, tix_ref, tiy_ref, tiz_ref, local, out_sem, z_send, z_recv, y_send, y_recv, i_send, i_recv,
+    par_ref, r8, rh, rl, tix_ref, tiy_ref, tiz_ref, local, out_sem, p_send, p_recv, i_send, i_recv,
 ):
     e = lax.axis_index("exp")
     t = lax.axis_index("tile")
@@ -88,14 +89,30 @@
     d_far = depth_of(yy, zh + side)
     t_to = lax.rem(t + 1 - 2 * half + tiles, tiles)
     t_from = lax.rem(t - 1 + 2 * half + tiles, tiles)
-    z_to = [(other, t, d_far), (e, t, d_far), (other, t, depth_of(yy, zh + 2))]
-    y_to = [(e, t, depth_of(yy + k, zh)) for k in range(1, 4)]
-    sources = [(other, t, d_far), (e, t, depth_of(yy, zh - side)), (other, t, depth_of(yy, zh + 2))]
-    sources += y_to + [(other, t, d), (e, t_from, d), (other, t_from, d)]
+    leads = lax.rem(t, 2) == 1
+    sibling = t + 1 - 2 * lax.rem(t, 2)
+    z_to = [(e, zh), (other, zh + side), (e, zh + side), (other, zh + 2)]
+    z_from = [(e, zh), (other, zh + side), (e, zh - side), (other, zh + 2)]
+    pairs = [(k, j) for k in range(4) for j in range(4) if k or j]
+    slab_to = [(z_to[k][0], t, depth_of(yy + j, z_to[k][1])) for k, j in pairs]
+    slab_from = [(z_from[k][0], t, depth_of(yy + 4 - j, z_from[k][1])) for k, j in pairs]
+    images_from = [(other, t, d), (other, t, d_far), (e, t_from, d), (other, t_from, d)]
 
     barrier = pltpu.get_barrier_semaphore()
-    for source in sources:
-        pl.semaphore_signal(barrier, inc=1, device_id=source, device_id_type=MESH)
+
+    def greet(devices):
+        for device in devices:
+            pl.semaphore_signal(barrier, inc=1, device_id=device, device_id_type=MESH)
+
+    @pl.when(leads)
+    def _():
+        greet(slab_from)
+
+    greet(images_from)
+
+    @pl.when(jnp.logical_not(leads))
+    def _():
+        greet([(e, sibling, d)])
 
     def lanes_of(depth):
         return pl.ds(pl.multiple_of(lax.rem(depth, 8) // 2 * LANES, LANES), LANES)
@@ -126,7 +143,9 @@
         for z in range(4):
             tile = jnp.where((row == z) & (cam == c), off_ref[c, z].astype(F32), tile)
             tile = jnp.where((row == z + 4) & (cam == c), frac_ref[c, z], tile)
-    par_ref[d] = tile
+    @pl.when(leads)
+    def _():
+        par_ref[d] = tile
 
     def remote(source, target, sends, recvs, index, device):
         return pltpu.make_async_remote_copy(
@@ -138,9 +157,9 @@
             device_id_type=MESH,
         )
 
-    along_z = [remote(par_ref.at[d], par_ref.at[d], z_send, z_recv, k, to) for k, to in enumerate(z_to)]
-    rows = pl.ds(pl.multiple_of(4 * yy, 4), 4)
-    along_y = [remote(par_ref.at[rows], par_ref.at[rows], y_send, y_recv, k, to) for k, to in enumerate(y_to)]
+    slabs = [remote(par_ref.at[d], par_ref.at[d], p_send, p_recv, k, to) for k, to in enumerate(slab_to)]
+    handed = remote(par_ref, par_ref, p_send, p_recv, 15, (e, sibling, d))
+
     pixels = [
         remote(own.at[:, strip_src, :], packed.at[e, :, strip_dst, :], i_send, i_recv, 0, (e, t_to, d)),
         remote(own.at[:, strip_src, :], packed.at[e, :, strip_dst, :], i_send, i_recv, 1, (other, t_to, d)),
@@ -148,9 +167,16 @@
         remote(far, packed.at[e, 1, main_dst, :], i_send, i_recv, 3, (other, t, d_far)),
     ]
 
-    pl.semaphore_wait(barrier, len(sources))
-    for copy in along_z:
-        copy.start()
+    @pl.when(leads)
+    def _():
+        pl.semaphore_wait(barrier, len(slab_to) + 5)
+        for copy in slabs:
+            copy.start()
+
+    @pl.when(jnp.logical_not(leads))
+    def _():
+        pl.semaphore_wait(barrier, 4)
+
 
     def pack(even, odd, high_half):
         low = iota(even.shape, 1) < BRICK
@@ -193,10 +219,6 @@
     for copy in results[:3]:
         copy.start()
 
-    for copy in along_z:
-        copy.wait_recv()
-    for copy in along_y:
-        copy.start()
     for copy in pixels:
         copy.wait_recv()
 
@@ -221,10 +243,24 @@
 
     for copy in results[3:6]:
         copy.start()
-    for copy in along_y:
-        copy.wait_recv()
+    @pl.when(leads)
+    def _():
+        for copy in slabs:
+            copy.wait_recv()
+        handed.start()
+
+    @pl.when(jnp.logical_not(leads))
+    def _():
+        handed.wait_recv()
+
     results[6].start()
-    for copy in along_z + along_y + pixels:
+
+    @pl.when(leads)
+    def _():
+        for copy in slabs + [handed]:
+            copy.wait_send()
+
+    for copy in pixels:
         copy.wait_send()
     for copy in results:
         copy.wait()
@@ -249,10 +285,8 @@
             *[pltpu.VMEM(shape, dtype) for shape, dtype in HANDED],
             pltpu.SemaphoreType.DMA((5,)),
             pltpu.SemaphoreType.DMA((len(HANDED),)),
-            pltpu.SemaphoreType.DMA((3,)),
-            pltpu.SemaphoreType.DMA((3,)),
-            pltpu.SemaphoreType.DMA((3,)),
-            pltpu.SemaphoreType.DMA((3,)),
+            pltpu.SemaphoreType.DMA((16,)),
+            pltpu.SemaphoreType.DMA((16,)),
             pltpu.SemaphoreType.DMA((4,)),
             pltpu.SemaphoreType.DMA((4,)),
         ],
@@ -360,8 +394,8 @@
     for x in range(0, BRICK, 2):
         volume = jnp.exp(dot(back, windows(uh, ul, x)))
         spec = dot(fz, stack_rows(volume))
-        zs[x * BRICK : (x + 1) * BRICK, :] = spec[:, :LANES]
-        zs[(x + 1) * BRICK : (x + 2) * BRICK, :] = spec[:, LANES:]
+        zs[x * STEP : x * STEP + BRICK, :] = spec[:, :LANES]
+        zs[(x + 1) * STEP : (x + 1) * STEP + BRICK, :] = spec[:, LANES:]
 
     ty = ty_ref[...]
     tix, tiy, tiz = tix_ref[...], tiy_ref[...], tiz_ref[...]
@@ -372,9 +406,9 @@
     row_zero = (iota((BRICK, LANES), 0) == 0) & (iota((BRICK, LANES), 1) % BRICK == 0)
 
     def load_plane(kz):
-        re = zs[pl.ds(kz, BRICK, stride=BRICK), :]
+        re = zs[pl.ds(kz, BRICK, stride=STEP), :]
         if 0 < kz < 32:
-            im = zs[pl.ds(32 + kz, BRICK, stride=BRICK), :]
+            im = zs[pl.ds(32 + kz, BRICK, stride=STEP), :]
         else:
             im = jnp.zeros_like(re)
         return jnp.concatenate([re, im], axis=1)
@@ -399,11 +433,11 @@
             part = back_x[:, k * LANES : (k + 1) * LANES]
             corr = part[:BRICK] + sign * pltpu.roll(part[BRICK:], BRICK, 1)
             even, odd_x = corr[: BRICK // 2], corr[BRICK // 2 :]
-            qs[pl.ds(kz, BRICK // 2, stride=BRICK), :] = jnp.where(
+            qs[pl.ds(kz, BRICK // 2, stride=STEP), :] = jnp.where(
                 low_quarter, even, pltpu.roll(odd_x, BRICK, 1)
             )
             if 0 < kz < 32:
-                qs[pl.ds(32 + kz, BRICK // 2, stride=BRICK), :] = jnp.where(
+                qs[pl.ds(32 + kz, BRICK // 2, stride=STEP), :] = jnp.where(
                     low_quarter, pltpu.roll(even, BRICK, 1), odd_x
                 )
 
@@ -419,7 +453,7 @@
     copies = []
     for x in range(BRICK // 4):
         data = jnp.concatenate(
-            [qs[BRICK * k : BRICK * (k + 1), :] for k in (2 * x, 2 * x + 1)], axis=1
+            [qs[STEP * k : STEP * k + BRICK, :] for k in (2 * x, 2 * x + 1)], axis=1
         )
         result[:, 2 * x * LANES : 2 * (x + 1) * LANES] = dot(tiz, stack_rows(data))
         if x % 4 == 3:
@@ -465,8 +499,8 @@
             pltpu.VMEM((8, COLS_U * LANES), F32),
             pltpu.VMEM((16, COLS_U * LANES), BF16),
             pltpu.VMEM((16, COLS_U * LANES), BF16),
-            pltpu.VMEM((BRICK * BRICK, LANES), F32),
-            pltpu.VMEM((BRICK * BRICK // 2, LANES), F32),
+            pltpu.VMEM((BRICK * STEP, LANES), F32),
+            pltpu.VMEM((BRICK // 2 * STEP, LANES), F32),
             pltpu.VMEM((BRICK // 2, BRICK * BRICK), F32),
             pltpu.SemaphoreType.DMA((4,)),
             pltpu.SemaphoreType.DMA((len(HANDED + TABLES),)),

time: 26.9 us -> 24.3 us (0.903)
  Pallas kernels: 26.6 us -> 23.9 us
    pallas_call x1, Pallas kernels: 16 us -> 14.5 us  [exchange(): pl.pallas_call(exchange_kernel, out_shape=[jax.ShapeDtypeStruct(shape, dt...]
    pallas_call x1, Pallas kernels: 10.6 us -> 9.38 us  [compute(): pl.pallas_call(compute_kernel, out_shape=jax.ShapeDtypeStruct((BRICK // 2...]
where the time goes in v5:
time: 24.3 us; the launch traced here: 23.9 us
  Pallas kernels  23.9 us (98%)
    pallas_call x1, Pallas kernels, exchange(): pl.pallas_call(exchange_kernel, out_shape=[jax.ShapeDtypeStruct(shape, dt...  14.5 us
    pallas_call x1, Pallas kernels, compute(): pl.pallas_call(compute_kernel, out_shape=jax.ShapeDtypeStruct((BRICK // 2...  9.38 us

profile of v5, /device:TPU:2, one launch (start us, length us, event | category | flops | bytes accessed | tf_op | source)
XLA Modules:
  0.0 23.9 jit_solution(12986139898945630675)
XLA Ops:
  0.0 14.5 %shard_map.73 = (f32[16,8,128]{2,1,0:T(8,128)}, f32[896,128]{1,0:T(8,128)}, bf16[16,14336]{1,0:T(8,128)(2,1)}, bf16[16,14336]{1,0:T(8,128)(2,1)}, bf16[128,192]{...) custom-call(s32[4,4]{1,0:T(4,128)} %off_hbm.1, f32[4,4]{1,0:T(4,128)} %frac_hbm.1, ...), custom_call_target="tpu_custom_call" | custom-call | tf_op jit(solution)/shard_map/pallas_call | solution.py:271
  14.5 9.4 %shard_map.74 = f32[32,4096]{1,0:T(8,128)} custom-call(f32[16,8,128]{2,1,0:T(8,128)} %get-tuple-element.12.refs_0_, f32[896,128]{1,0:T(8,128)} %get-tuple-element.13.refs_1_, bf16[16,14336]{1,0:T(8,128)(2,1)} %get-tuple-element.14.refs_2_, bf16[16,14336]{1,0:T(8,128)(2,1)} %get-tuple-element.15.refs_3_, bf16[128,192]{1,0:T(8,128)(2,1)} %get-tuple-element.16.refs_4_, ...), custom_call_target="tpu_custom_call" | custom-call | tf_op jit(solution)/shard_map/pallas_call | solution.py:491

commit v6 on v5

--- a/solution.py
+++ b/solution.py
@@ -70,9 +70,9 @@
 
 
 def exchange_kernel(
-    off_hbm, frac_hbm, shift_hbm, img_ref, par_out, r8_out, rh_out, rl_out, tix_out, tiy_out, tiz_out,
-    off_ref, frac_ref, shift_ref, stage, stage_far, own, far, packed,
-    par_ref, r8, rh, rl, tix_ref, tiy_ref, tiz_ref, local, out_sem, p_send, p_recv, i_send, i_recv,
+    off_hbm, frac_hbm, shift_hbm, img_ref, fz_hbm, ty_hbm, cs_hbm, out_ref, off_ref, frac_ref, shift_ref, stage, stage_far, own, far, packed,
+    par_ref, r8, rh, rl, tix_ref, tiy_ref, tiz_ref, fz_ref, ty_ref, cs_ref,
+    g, a8, uh, ul, zs, qs, result, done, local, p_send, p_recv, i_send, i_recv,
 ):
     e = lax.axis_index("exp")
     t = lax.axis_index("tile")
@@ -131,7 +131,11 @@
         pltpu.make_async_copy(img_ref.at[0, :, :, lanes_of(d)], stage, local.at[3]),
         pltpu.make_async_copy(img_ref.at[0, pl.ds(2, 2), main_src, lanes_of(d_far)], stage_far, local.at[4]),
     ]
-    for copy in small + large:
+    constants = [
+        pltpu.make_async_copy(source, target, local.at[5 + k])
+        for k, (source, target) in enumerate([(fz_hbm, fz_ref), (ty_hbm, ty_ref), (cs_hbm, cs_ref)])
+    ]
+    for copy in small + large + constants:
         copy.start()
     small[0].wait()
     small[1].wait()
@@ -209,15 +213,6 @@
     kz = jnp.where(c > 32, c - 32, c)
     weight = jnp.where((kz == 0) | (kz == 32), 1.0, 2.0)
     tiz_ref[...] = twice(weight * turn_cos(kz * (r + 32 * e + sz) + jnp.where(c > 32, 16, 0)))
-
-    results = [
-        pltpu.make_async_copy(source, target, out_sem.at[k])
-        for k, (source, target) in enumerate(
-            [(tix_ref, tix_out), (tiy_ref, tiy_out), (tiz_ref, tiz_out), (r8, r8_out), (rh, rh_out), (rl, rl_out), (par_ref, par_out)]
-        )
-    ]
-    for copy in results[:3]:
-        copy.start()
 
     for copy in pixels:
         copy.wait_recv()
@@ -241,8 +236,6 @@
         rh[:, x * LANES : (x + 1) * LANES] = high
         rl[:, x * LANES : (x + 1) * LANES] = lows
 
-    for copy in results[3:6]:
-        copy.start()
     @pl.when(leads)
     def _():
         for copy in slabs:
@@ -253,7 +246,12 @@
     def _():
         handed.wait_recv()
 
-    results[6].start()
+    for copy in constants:
+        copy.wait()
+    compute_part(
+        out_ref, par_ref, r8, rh, rl, tix_ref, tiy_ref, tiz_ref, fz_ref, ty_ref, cs_ref,
+        g, a8, uh, ul, zs, qs, result, done,
+    )
 
     @pl.when(leads)
     def _():
@@ -262,55 +260,12 @@
 
     for copy in pixels:
         copy.wait_send()
-    for copy in results:
-        copy.wait()
-
-
-def exchange(images, offsets, fractions, shifts):
-    hbm = pl.BlockSpec(memory_space=pltpu.HBM)
-    return pl.pallas_call(
-        exchange_kernel,
-        out_shape=[jax.ShapeDtypeStruct(shape, dtype) for shape, dtype in HANDED],
-        in_specs=[hbm] * 4,
-        out_specs=[hbm] * 7,
-        scratch_shapes=[
-            pltpu.SMEM((4, 4), jnp.int32),
-            pltpu.SMEM((4, 4), F32),
-            pltpu.SMEM((1, 3), jnp.int32),
-            pltpu.VMEM((4, 2 * BRICK, LANES), F32),
-            pltpu.VMEM((2, MAIN, LANES), F32),
-            pltpu.VMEM((2, 2 * BRICK, LANES), F32),
-            pltpu.VMEM((MAIN, LANES), F32),
-            pltpu.VMEM((2, 2, COLS_R, LANES), F32),
-            *[pltpu.VMEM(shape, dtype) for shape, dtype in HANDED],
-            pltpu.SemaphoreType.DMA((5,)),
-            pltpu.SemaphoreType.DMA((len(HANDED),)),
-            pltpu.SemaphoreType.DMA((16,)),
-            pltpu.SemaphoreType.DMA((16,)),
-            pltpu.SemaphoreType.DMA((4,)),
-            pltpu.SemaphoreType.DMA((4,)),
-        ],
-        compiler_params=pltpu.CompilerParams(
-            collective_id=0, has_side_effects=True, vmem_limit_bytes=VMEM_LIMIT
-        ),
-    )(offsets, fractions, shifts, images)
-
-
-def compute_kernel(
-    *refs
+
+
+def compute_part(
+    out_ref, par_ref, r8, rh, rl, tix_ref, tiy_ref, tiz_ref, fz_ref, ty_ref, cs_ref,
+    g, a8, uh, ul, zs, qs, result, done,
 ):
-    count = len(HANDED + TABLES)
-    out_ref = refs[count]
-    g, a8, uh, ul, zs, qs, result, done, loaded = refs[2 * count + 1 :]
-    loads = [
-        pltpu.make_async_copy(refs[k], refs[count + 1 + k], loaded.at[k]) for k in range(count)
-    ]
-    order = (0, 2, 3, 1, 7, 8, 9, 4, 5, 6)
-    for k in order:
-        loads[k].start()
-    par_ref, r8, rh, rl, tix_ref, tiy_ref, tiz_ref, fz_ref, ty_ref, cs_ref = refs[count + 1 : 2 * count + 1]
-    loads[0].wait()
-
     sub = iota((8, LANES), 0)
     offs, fracs = [], []
     for i in range(PEERS // 2):
@@ -343,9 +298,6 @@
     lift = jnp.sum(weights * jnp.log(by_lane[0:1]), axis=1, keepdims=True) * 0.5
     lift = jnp.broadcast_to(lift, (BRICK, 2 * LANES))
 
-    for k in order[1:]:
-        loads[k].wait()
-
     def windows(high_ref, low_ref, x):
         def of(ref):
             return [ref[:, (x + 1 + 4 * q) * LANES : (x + 3 + 4 * q) * LANES] for q in range(4)]
@@ -486,14 +438,22 @@
     return fz, ty, cs
 
 
-def compute(*exchanged):
+def per_device(images, offsets, fractions, shifts):
     hbm = pl.BlockSpec(memory_space=pltpu.HBM)
-    return pl.pallas_call(
-        compute_kernel,
+    result = pl.pallas_call(
+        exchange_kernel,
         out_shape=jax.ShapeDtypeStruct((BRICK // 2, BRICK * BRICK), F32),
-        in_specs=[hbm] * len(HANDED + TABLES),
+        in_specs=[hbm] * 7,
         out_specs=hbm,
         scratch_shapes=[
+            pltpu.SMEM((4, 4), jnp.int32),
+            pltpu.SMEM((4, 4), F32),
+            pltpu.SMEM((1, 3), jnp.int32),
+            pltpu.VMEM((4, 2 * BRICK, LANES), F32),
+            pltpu.VMEM((2, MAIN, LANES), F32),
+            pltpu.VMEM((2, 2 * BRICK, LANES), F32),
+            pltpu.VMEM((MAIN, LANES), F32),
+            pltpu.VMEM((2, 2, COLS_R, LANES), F32),
             *[pltpu.VMEM(shape, dtype) for shape, dtype in HANDED + TABLES],
             pltpu.VMEM((BRICK, COLS_V * LANES), F32),
             pltpu.VMEM((8, COLS_U * LANES), F32),
@@ -503,14 +463,17 @@
             pltpu.VMEM((BRICK // 2 * STEP, LANES), F32),
             pltpu.VMEM((BRICK // 2, BRICK * BRICK), F32),
             pltpu.SemaphoreType.DMA((4,)),
-            pltpu.SemaphoreType.DMA((len(HANDED + TABLES),)),
+            pltpu.SemaphoreType.DMA((8,)),
+            pltpu.SemaphoreType.DMA((16,)),
+            pltpu.SemaphoreType.DMA((16,)),
+            pltpu.SemaphoreType.DMA((4,)),
+            pltpu.SemaphoreType.DMA((4,)),
         ],
-        compiler_params=pltpu.CompilerParams(vmem_limit_bytes=VMEM_LIMIT),
-    )(*exchanged, *[jnp.asarray(table) for table in tables()])
-
-
-def per_device(images, offsets, fractions, shifts):
-    return compute(*exchange(images, offsets, fractions, shifts))[None]
+        compiler_params=pltpu.CompilerParams(
+            collective_id=0, has_side_effects=True, vmem_limit_bytes=VMEM_LIMIT
+        ),
+    )(offsets, fractions, shifts, images, *[jnp.asarray(table) for table in tables()])
+    return result[None]
 
 
 def solution(mesh):

time: 24.3 us -> 24 us (0.988); the launches traced: 23.9 us -> 23.9 us
  Pallas kernels: 23.9 us -> 22 us
  local copies, waits for them, and re-layouts: 0 us -> 1.87 us
    unnamed x0 -> x1, local copies, waits for them, and re-layouts: none -> 1.87 us
    pallas_call x2 -> x1, Pallas kernels: 23.9 us -> 22 us  [per_device(): pl.pallas_call(exchange_kernel, out_shape=jax.ShapeDtypeStruct((BRICK //...]
where the time goes in v6:
time: 24 us; the launch traced here: 23.9 us
  Pallas kernels  22 us (92%)
  local copies, waits for them, and re-layouts  1.87 us (8%)
    pallas_call x1, Pallas kernels, per_device(): pl.pallas_call(exchange_kernel, out_shape=jax.ShapeDtypeStruct((BRICK //...  22 us
    unnamed x1, local copies, waits for them, and re-layouts  1.87 us

profile of v6, /device:TPU:2, one launch (start us, length us, event | category | flops | bytes accessed | tf_op | source)
XLA Modules:
  0.0 23.9 jit_solution(14088857754637999814)
XLA Ops:
  0.0 22.0 %shard_map.73 = f32[32,4096]{1,0:T(8,128)} custom-call(s32[4,4]{1,0:T(4,128)} %off_hbm.1, f32[4,4]{1,0:T(4,128)} %frac_hbm.1, s32[1,3]{1,0:T(1,128)} %shift_hbm.1, f32[1,4,128,512]{3,2,1,0:T(8,128)} %img_ref.1, bf16[64,192]{1,0:T(8,128)(2,1)} %constant.6.clone.fz_hbm, bf16[768,256]{1,0:T(8,128)(2,1)} %constant.7.clone.ty_hbm, ...), custom_call_target="tpu_custom_call" | custom-call | tf_op jit(solution)/shard_map/pallas_call | solution.py:443
  22.0 1.9 %copy.9 = f32[1,32,4096]{2,1,0:T(8,128)} copy(f32[1,32,4096]{2,1,0:T(8,128)} %bitcast.1) | data formatting | bytes 1048576

commit v7 on v6

--- a/solution.py
+++ b/solution.py
@@ -93,7 +93,7 @@
     sibling = t + 1 - 2 * lax.rem(t, 2)
     z_to = [(e, zh), (other, zh + side), (e, zh + side), (other, zh + 2)]
     z_from = [(e, zh), (other, zh + side), (e, zh - side), (other, zh + 2)]
-    pairs = [(k, j) for k in range(4) for j in range(4) if k or j]
+    pairs = sorted([(k, j) for k in range(4) for j in range(4) if k or j], key=lambda p: -p[0] - min(p[1], 4 - p[1]))
     slab_to = [(z_to[k][0], t, depth_of(yy + j, z_to[k][1])) for k, j in pairs]
     slab_from = [(z_from[k][0], t, depth_of(yy + 4 - j, z_from[k][1])) for k, j in pairs]
     images_from = [(other, t, d), (other, t, d_far), (e, t_from, d), (other, t_from, d)]

time: 24 us -> 23.9 us (level); the launches traced: 23.9 us -> 23.4 us
  Pallas kernels: 22 us -> 21.6 us
    pallas_call x1, Pallas kernels: 22 us -> 21.6 us  [per_device(): pl.pallas_call(exchange_kernel, out_shape=jax.ShapeDtypeStruct((BRICK //...]
where the time goes in v7:
time: 23.9 us; the launch traced here: 23.4 us
  Pallas kernels  21.6 us (90%)
  local copies, waits for them, and re-layouts  1.87 us (8%)
    pallas_call x1, Pallas kernels, per_device(): pl.pallas_call(exchange_kernel, out_shape=jax.ShapeDtypeStruct((BRICK //...  21.6 us
    unnamed x1, local copies, waits for them, and re-layouts  1.87 us

profile of v7, /device:TPU:2, one launch (start us, length us, event | category | flops | bytes accessed | tf_op | source)
XLA Modules:
  0.0 23.4 jit_solution(3986928939010524080)
XLA Ops:
  0.0 21.6 %shard_map.73 = f32[32,4096]{1,0:T(8,128)} custom-call(s32[4,4]{1,0:T(4,128)} %off_hbm.1, f32[4,4]{1,0:T(4,128)} %frac_hbm.1, s32[1,3]{1,0:T(1,128)} %shift_hbm.1, f32[1,4,128,512]{3,2,1,0:T(8,128)} %img_ref.1, bf16[64,192]{1,0:T(8,128)(2,1)} %constant.6.clone.fz_hbm, bf16[768,256]{1,0:T(8,128)(2,1)} %constant.7.clone.ty_hbm, ...), custom_call_target="tpu_custom_call" | custom-call | tf_op jit(solution)/shard_map/pallas_call | solution.py:443
  21.6 1.9 %copy.9 = f32[1,32,4096]{2,1,0:T(8,128)} copy(f32[1,32,4096]{2,1,0:T(8,128)} %bitcast.1) | data formatting | bytes 1048576

commit v8 on v7

--- a/solution.py
+++ b/solution.py
@@ -98,35 +98,37 @@
     slab_from = [(z_from[k][0], t, depth_of(yy + 4 - j, z_from[k][1])) for k, j in pairs]
     images_from = [(other, t, d), (other, t, d_far), (e, t_from, d), (other, t_from, d)]
 
-    barrier = pltpu.get_barrier_semaphore()
-
-    def greet(devices):
-        for device in devices:
-            pl.semaphore_signal(barrier, inc=1, device_id=device, device_id_type=MESH)
-
-    @pl.when(leads)
-    def _():
-        greet(slab_from)
-
-    greet(images_from)
-
-    @pl.when(jnp.logical_not(leads))
-    def _():
-        greet([(e, sibling, d)])
-
-    def lanes_of(depth):
-        return pl.ds(pl.multiple_of(lax.rem(depth, 8) // 2 * LANES, LANES), LANES)
-
-    main_src = pl.ds(pl.multiple_of((BRICK - EDGE) * half, 8), MAIN)
-    main_dst = pl.ds(pl.multiple_of(EDGE * (1 - half), 8), MAIN)
-    strip_src = pl.ds(pl.multiple_of((2 * BRICK - EDGE) * (1 - half), 8), EDGE)
-    strip_dst = pl.ds(pl.multiple_of(MAIN * half, 8), EDGE)
-
     small = [
         pltpu.make_async_copy(off_hbm, off_ref, local.at[0]),
         pltpu.make_async_copy(frac_hbm, frac_ref, local.at[1]),
         pltpu.make_async_copy(shift_hbm, shift_ref, local.at[2]),
     ]
+    for copy in small:
+        copy.start()
+    barrier = pltpu.get_barrier_semaphore()
+
+    def greet(devices):
+        for device in devices:
+            pl.semaphore_signal(barrier, inc=1, device_id=device, device_id_type=MESH)
+
+    @pl.when(leads)
+    def _():
+        greet(slab_from)
+
+    greet(images_from)
+
+    @pl.when(jnp.logical_not(leads))
+    def _():
+        greet([(e, sibling, d)])
+
+    def lanes_of(depth):
+        return pl.ds(pl.multiple_of(lax.rem(depth, 8) // 2 * LANES, LANES), LANES)
+
+    main_src = pl.ds(pl.multiple_of((BRICK - EDGE) * half, 8), MAIN)
+    main_dst = pl.ds(pl.multiple_of(EDGE * (1 - half), 8), MAIN)
+    strip_src = pl.ds(pl.multiple_of((2 * BRICK - EDGE) * (1 - half), 8), EDGE)
+    strip_dst = pl.ds(pl.multiple_of(MAIN * half, 8), EDGE)
+
     large = [
         pltpu.make_async_copy(img_ref.at[0, :, :, lanes_of(d)], stage, local.at[3]),
         pltpu.make_async_copy(img_ref.at[0, pl.ds(2, 2), main_src, lanes_of(d_far)], stage_far, local.at[4]),
@@ -135,7 +137,7 @@
         pltpu.make_async_copy(source, target, local.at[5 + k])
         for k, (source, target) in enumerate([(fz_hbm, fz_ref), (ty_hbm, ty_ref), (cs_hbm, cs_ref)])
     ]
-    for copy in small + large + constants:
+    for copy in large + constants:
         copy.start()
     small[0].wait()
     small[1].wait()

time: 23.9 us -> 23.9 us (level)
  no operation moved by 1% of the time
where the time goes in v8:
time: 23.9 us; the launch traced here: 23.5 us
  Pallas kernels  21.6 us (90%)
  local copies, waits for them, and re-layouts  1.87 us (8%)
    pallas_call x1, Pallas kernels, per_device(): pl.pallas_call(exchange_kernel, out_shape=jax.ShapeDtypeStruct((BRICK //...  21.6 us
    unnamed x1, local copies, waits for them, and re-layouts  1.87 us

profile of v8, /device:TPU:2, one launch (start us, length us, event | category | flops | bytes accessed | tf_op | source)
XLA Modules:
  0.0 23.5 jit_solution(16024474362292525145)
XLA Ops:
  0.0 21.6 %shard_map.73 = f32[32,4096]{1,0:T(8,128)} custom-call(s32[4,4]{1,0:T(4,128)} %off_hbm.1, f32[4,4]{1,0:T(4,128)} %frac_hbm.1, s32[1,3]{1,0:T(1,128)} %shift_hbm.1, f32[1,4,128,512]{3,2,1,0:T(8,128)} %img_ref.1, bf16[64,192]{1,0:T(8,128)(2,1)} %constant.6.clone.fz_hbm, bf16[768,256]{1,0:T(8,128)(2,1)} %constant.7.clone.ty_hbm, ...), custom_call_target="tpu_custom_call" | custom-call | tf_op jit(solution)/shard_map/pallas_call | solution.py:445
  21.6 1.9 %copy.9 = f32[1,32,4096]{2,1,0:T(8,128)} copy(f32[1,32,4096]{2,1,0:T(8,128)} %bitcast.1) | data formatting | bytes 1048576
